TPU v7x, 128 devices: a whole 4x4x4 slice. The times are simulated.
128 devices in a mesh: region: 8 (over z_lo, y), sub: 16 (over z_hi, x, core).
Axes of the slice: x: 4, y: 4, z: 4 (z_hi: 2, z_lo: 2; z = z_hi * 2 + z_lo), core: 2. Of those that a mesh axis runs over, the one named last changes fastest.
Arguments:
- node_feats: bfloat16 [131072, 512], P(('region', 'sub')), may hold values from -6 to 6
- gain_in: float32 [512], replicated, may hold values from 0.25 to 1.75
- w_qkv: bfloat16 [512, 1536], replicated, may hold values from -4 to 4
- gain_out: float32 [512], replicated, may hold values from 0.25 to 1.75
- w_out: bfloat16 [512, 512], replicated, may hold values from -0.25 to 0.25
- adjacency: int32 [2048, 7], P(('region', 'sub')), may hold values from 0 to 2047, as said below
- fine_valid: int32 [2048, 7], P(('region', 'sub')), may hold values 0 or 1
- coarse_mask: int32 [2048, 40], P(('region', 'sub')), may hold values 0 or 1
- coarse_src: int32 [2560], P(('region', 'sub')), may hold values from 0 to 131071, as said below
Outputs:
- update: bfloat16 [131072, 512], P(('region', 'sub'))
Inputs may be any that keep to these rules, and one draw needn't show every extreme that they name: `adjacency`: entry (b, 0) is b itself. Block b is held by device d = b // 16, devices numbered region * 16 + sub; every entry of row b names a block held by d or by a device one step away along region or along sub. `coarse_src`: entry i names a node held by the device that holds entry i: a node from (i // 20) * 16 * 64 to that plus 16 * 64 - 1.
All inputs are finite; a program needn't handle non-finite values. No bound on the sum of `fine_valid` or of `coarse_mask` on one device may be relied on, other than what follows from the above.
Results may differ from a plain program's by a relative error of at most 0.0083.
Values may be sent and summed in bfloat16 or wider, within the bound.
A program may use at most 128 MiB of HBM per device.

v0:
```python
import math

import jax
import jax.numpy as jnp
from jax import lax
from jax.sharding import PartitionSpec as P

D = 512
HEADS = 8
BLOCK = 64
NADJ = 7


neg_large = -1e30


def passed_along(block, axis, distance):
    devices = range(lax.axis_size(axis))
    route = [(i - distance, i) for i in devices if i - distance in devices]
    return lax.ppermute(block, axis, route)


def rms_scale(feats, gain):
    vals = feats.astype(jnp.float32)
    mean_square = jnp.mean(vals * vals, axis=-1, keepdims=True)
    return (vals * lax.rsqrt(mean_square + 1e-06) * gain).astype(jnp.bfloat16)


def per_device(
    node_feats, gain_in, w_qkv, gain_out, w_out, adjacency, fine_valid, coarse_mask, coarse_src
):
    row_count = node_feats.shape[0]
    blocks = row_count // BLOCK
    head_width = D // HEADS
    score_scale = head_width ** (-0.5)
    normed = rms_scale(node_feats, gain_in)
    projected = jnp.dot(normed, w_qkv, preferred_element_type=jnp.float32).astype(jnp.bfloat16)
    key_value = projected[:, D:]
    sub_count = lax.axis_size("sub")
    device_pos = lax.axis_index("region") * sub_count + lax.axis_index("sub")
    local_src = coarse_src - device_pos * row_count
    coarse_kv = lax.all_gather(key_value[local_src], ("region", "sub"), axis=0, tiled=True)
    region_side = [passed_along(key_value, "region", offset) for offset in (1, -1)]
    sub_side = [passed_along(key_value, "sub", offset) for offset in (1, -1)]
    window = jnp.concatenate([key_value] + region_side + sub_side, axis=0)
    window = window.reshape(5 * blocks, BLOCK, 2 * D)
    neighbour_dev = adjacency // blocks
    local_blk = adjacency % blocks
    dev_gap = neighbour_dev - device_pos
    direction = jnp.where(
        dev_gap == -sub_count,
        1,
        jnp.where(
            dev_gap == sub_count, 2, jnp.where(dev_gap == -1, 3, jnp.where(dev_gap == 1, 4, 0))
        ),
    )
    slot_index = direction * blocks + local_blk
    slot_live = (fine_valid == 1) | (jnp.arange(NADJ)[None, :] == 0)
    group_size = math.gcd(blocks, 4)
    group_count = blocks // group_size
    queries = projected[:, :D].reshape(group_count, group_size, BLOCK, D)
    group_slots = slot_index.reshape(group_count, group_size, NADJ)
    group_live = slot_live.reshape(group_count, group_size, NADJ)
    group_coarse = coarse_mask.reshape(group_count, group_size, coarse_mask.shape[1])
    lane_width = min(128, D)
    heads_per_lane = lane_width // head_width
    lane_head = jnp.arange(lane_width) // head_width

    def one_group(inputs):
        block_q, slots, live_slots, coarse_live = inputs
        fine_kv = window[slots].reshape(group_size, NADJ * BLOCK, 2 * D)
        fine_open = jnp.repeat(live_slots, BLOCK, axis=1)[:, None, :]
        coarse_open = jnp.repeat(coarse_live == 1, BLOCK, axis=1)[:, None, :]
        pieces = []
        for lane_start in range(0, D, lane_width):
            lane_query = block_q[..., lane_start : lane_start + lane_width]
            fine_keys = fine_kv[..., lane_start : lane_start + lane_width]
            fine_values = fine_kv[..., D + lane_start : D + lane_start + lane_width]
            coarse_keys = coarse_kv[:, lane_start : lane_start + lane_width]
            coarse_values = coarse_kv[:, D + lane_start : D + lane_start + lane_width]
            merged = None
            for sub_head in range(heads_per_lane):
                own_lanes = lane_head == sub_head
                head_query = jnp.where(own_lanes, lane_query, jnp.zeros((), jnp.bfloat16))
                fine_scores = (
                    jnp.einsum(
                        "gqc,gkc->gqk", head_query, fine_keys, preferred_element_type=jnp.float32
                    )
                    * score_scale
                )
                fine_scores = jnp.where(fine_open, fine_scores, neg_large)
                coarse_scores = (
                    jnp.einsum(
                        "gqc,kc->gqk", head_query, coarse_keys, preferred_element_type=jnp.float32
                    )
                    * score_scale
                )
                coarse_scores = jnp.where(coarse_open, coarse_scores, neg_large)
                score_peak = jnp.maximum(
                    jnp.max(fine_scores, axis=-1), jnp.max(coarse_scores, axis=-1)
                )[..., None]
                fine_exp = jnp.exp(fine_scores - score_peak)
                coarse_exp = jnp.exp(coarse_scores - score_peak)
                total = jnp.sum(fine_exp, axis=-1, keepdims=True) + jnp.sum(
                    coarse_exp, axis=-1, keepdims=True
                )
                fine_weights = (fine_exp / total).astype(jnp.bfloat16)
                coarse_weights = (coarse_exp / total).astype(jnp.bfloat16)
                head_out = jnp.einsum(
                    "gqk,gkc->gqc", fine_weights, fine_values, preferred_element_type=jnp.float32
                )
                head_out = head_out + jnp.einsum(
                    "gqk,kc->gqc", coarse_weights, coarse_values, preferred_element_type=jnp.float32
                )
                merged = head_out if merged is None else jnp.where(own_lanes, head_out, merged)
            pieces.append(merged)
        mixed_out = jnp.concatenate(pieces, axis=-1)
        return mixed_out.reshape(group_size * BLOCK, D).astype(jnp.bfloat16)

    attended = lax.map(one_group, (queries, group_slots, group_live, group_coarse)).reshape(
        row_count, D
    )
    renormed = rms_scale(attended, gain_out)
    return jnp.dot(renormed, w_out, preferred_element_type=jnp.float32).astype(jnp.bfloat16)


def solution(mesh):
    in_specs = (
        P(("region", "sub"), None),
        P(),
        P(),
        P(),
        P(),
        P(("region", "sub"), None),
        P(("region", "sub"), None),
        P(("region", "sub"), None),
        P(("region", "sub")),
    )
    out_specs = P(("region", "sub"), None)
    return jax.shard_map(
        per_device, mesh=mesh, in_specs=in_specs, out_specs=out_specs, check_vma=False
    )
```

profile of v0, /device:TPU:2, one launch (start us, length us, event | category | flops | bytes accessed | tf_op | source)
XLA Modules:
  0.0 443.0 jit_solution(15304550729839204200)
XLA Ops:
  6.5 1.6 fusion.147
  8.3 3.1 convolution_convert_fusion
  11.4 1.7 copy-done.3
  13.1 1.9 fusion.174
  16.3 4.8 %collective-permute-start = (bf16[1024,1024]{1,0:T(8,128)(2,1)S(1)}, bf16[1024,1024]{1,0:T(8,128)(2,1)}, u32[]{:S(2)}, u32[]{:S(2)}) collective-permute-start(bf16[1024,1024]{1,0:T(8,128)(2,1)S(1)} %get-tuple-element.186), channel_id=1, source_target_pairs={{0,16},{16,32},{32,48},{48,64},{64,80},{80,96},{96,112},{1,17},{17... | collective-permute-start | bytes 6291464 | tf_op jit(solution)/shard_map/ppermute | solution.py:20
  22.4 1.9 collective-permute-start.2
  24.3 3.6 collective-permute-start.3
  28.2 36.5 %collective-permute-done = bf16[1024,1024]{1,0:T(8,128)(2,1)} collective-permute-done((bf16[1024,1024]{1,0:T(8,128)(2,1)S(1)}, bf16[1024,1024]{1,0:T(8,128)(2,1)}, u32[]{:S(2)}, u32[]{:S(2)}) %collective-permute-start) | collective-permute-done | bytes 2097184 | tf_op jit(solution)/shard_map/ppermute | solution.py:20
  64.6 3.1 constant_dynamic-update-slice_fusion.3
  67.7 2.5 collective-permute-done.1
  70.1 3.1 constant_dynamic-update-slice_fusion.2
  73.2 3.1 constant_dynamic-update-slice_fusion.1
  76.3 3.2 constant_dynamic-update-slice_fusion
  79.5 197.9 %all-gather.4.cloned.1.call-done = bf16[128,20,1024]{2,1,0:T(8,128)(2,1)} async-done(((bf16[1,20,1024]{2,1,0:T(8,128)(2,1)}), bf16[128,20,1024]{2,1,0:T(8,128)(2,1)}) %all-gather.4.cloned.1.call-update) | async-done | bytes 5242896 | tf_op jit(solution)/shard_map/all_gather | solution.py:42
  277.4 9.0 %reshape.215 = bf16[2560,1024]{1,0:T(8,128)(2,1)} reshape(bf16[128,20,1024]{2,1,0:T(8,128)(2,1)} %all-gather.4.cloned.1.call-done) | data formatting | bytes 10485760
  286.5 144.8 %while.12 = (s32[]{:T(128)}, bf16[4,256,512]{2,1,0:T(8,128)(2,1)}, pred[4,4,7]{2,1,0:T(4,128)(4,1)S(1)}, bf16[4,4,64,512]{3,2,1,0:T(8,128)(2,1)S(1)}, s32[4,4,7]...) while((s32[]{:T(128)}, bf16[4,256,512]{2,1,0:T(8,128)(2,1)}, ...), condition=%wide.region_34.35_spmd.clone.clone, body=%wide.region_1.34_spmd.clone.clone.sunk | while | flops 3205495296 | bytes 144229808 | solution.py:120
  287.5 1.7 fusion.256
  289.3 6.7 %gather_fusion = bf16[28,64,1024]{2,1,0:T(8,128)(2,1)} fusion(bf16[80,64,1024]{2,1,0:T(8,128)(2,1)} %get-tuple-element.328, s32[1024]{0:T(1024)S(1)} %pad_clamp_fusion.3), kind=kCustom, calls=%fused_computation.clone.clone.1 | custom fusion | bytes 7340144 | tf_op jit(solution)/shard_map/while/body/eval_jaxpr/gather | solution.py:71
  298.4 2.1 fusion.260
  323.7 1.7 fusion.256
  325.5 6.7 %gather_fusion = bf16[28,64,1024]{2,1,0:T(8,128)(2,1)} fusion(bf16[80,64,1024]{2,1,0:T(8,128)(2,1)} %get-tuple-element.328, s32[1024]{0:T(1024)S(1)} %pad_clamp_fusion.3), kind=kCustom, calls=%fused_computation.clone.clone.1 | custom fusion | bytes 7340144 | tf_op jit(solution)/shard_map/while/body/eval_jaxpr/gather | solution.py:71
  332.4 1.4 fusion.257
  334.6 2.1 fusion.260
  359.9 1.7 fusion.256
  361.7 6.7 %gather_fusion = bf16[28,64,1024]{2,1,0:T(8,128)(2,1)} fusion(bf16[80,64,1024]{2,1,0:T(8,128)(2,1)} %get-tuple-element.328, s32[1024]{0:T(1024)S(1)} %pad_clamp_fusion.3), kind=kCustom, calls=%fused_computation.clone.clone.1 | custom fusion | bytes 7340144 | tf_op jit(solution)/shard_map/while/body/eval_jaxpr/gather | solution.py:71
  370.8 2.1 fusion.260
  396.1 1.7 fusion.256
  397.9 6.7 %gather_fusion = bf16[28,64,1024]{2,1,0:T(8,128)(2,1)} fusion(bf16[80,64,1024]{2,1,0:T(8,128)(2,1)} %get-tuple-element.328, s32[1024]{0:T(1024)S(1)} %pad_clamp_fusion.3), kind=kCustom, calls=%fused_computation.clone.clone.1 | custom fusion | bytes 7340144 | tf_op jit(solution)/shard_map/while/body/eval_jaxpr/gather | solution.py:71
  407.0 2.1 fusion.260
  431.2 1.7 multiply_reduce_fusion
  432.9 1.5 fusion.151
  434.5 1.7 convolution_convert_fusion.1
  (377 shorter events, 103.4 us)
Async XLA Ops:
  6.5 1.7 copy-start
  6.5 270.9 %all-gather.4.cloned.1.call-start = ((), (), s32[]{:S(2)}) async-start(), calls=%async_computation | async-start | bytes 6340608 | tf_op jit(solution)/shard_map/all_gather | solution.py:42
  11.3 1.7 copy-start.3
  13.1 1.9 copy-start.10
  13.1 14.9 %copy-start.6 = (s32[16,7]{0,1:T(8,128)S(1)}, s32[16,7]{0,1:T(8,128)}, u32[]{:S(2)}) copy-start(s32[16,7]{0,1:T(8,128)} %param.17) | copy-start | bytes 1348
  15.0 13.0 %copy-start.7 = (s32[16,7]{0,1:T(8,128)S(1)}, s32[16,7]{0,1:T(8,128)}, u32[]{:S(2)}) copy-start(s32[16,7]{0,1:T(8,128)} %param.16) | copy-start | bytes 1348
  16.3 48.4 %collective-permute-start = (bf16[1024,1024]{1,0:T(8,128)(2,1)S(1)}, bf16[1024,1024]{1,0:T(8,128)(2,1)}, u32[]{:S(2)}, u32[]{:S(2)}) collective-permute-start(bf16[1024,1024]{1,0:T(8,128)(2,1)S(1)} %get-tuple-element.186), channel_id=1, source_target_pairs={{0,16},{16,32},{32,48},{48,64},{64,80},{80,96},{96,112},{1,17},{17... | collective-permute-start | bytes 6291464 | tf_op jit(solution)/shard_map/ppermute | solution.py:20
  21.1 49.1 %collective-permute-start.1 = (bf16[1024,1024]{1,0:T(8,128)(2,1)S(1)}, bf16[1024,1024]{1,0:T(8,128)(2,1)}, u32[]{:S(2)}, u32[]{:S(2)}) collective-permute-start(bf16[1024,1024]{1,0:T(8,128)(2,1)S(1)} %get-tuple-element.186), channel_id=1, source_target_pairs={{16,0},{32,16},{48,32},{64,48},{80,64},{96,80},{112,96},{17,1},{33... | collective-permute-start | bytes 6291464 | tf_op jit(solution)/shard_map/ppermute | solution.py:20
  22.4 50.9 %collective-permute-start.2 = (bf16[1024,1024]{1,0:T(8,128)(2,1)S(1)}, bf16[1024,1024]{1,0:T(8,128)(2,1)}, u32[]{:S(2)}, u32[]{:S(2)}) collective-permute-start(bf16[1024,1024]{1,0:T(8,128)(2,1)S(1)} %get-tuple-element.186), channel_id=1, source_target_pairs={{0,1},{1,2},{2,3},{3,4},{4,5},{5,6},{6,7},{7,8},{8,9},{9,10},{10,1... | collective-permute-start | bytes 6291464 | tf_op jit(solution)/shard_map/ppermute | solution.py:20
  24.3 52.1 %collective-permute-start.3 = (bf16[1024,1024]{1,0:T(8,128)(2,1)S(1)}, bf16[1024,1024]{1,0:T(8,128)(2,1)}, u32[]{:S(2)}, u32[]{:S(2)}) collective-permute-start(bf16[1024,1024]{1,0:T(8,128)(2,1)S(1)} %get-tuple-element.186), channel_id=1, source_target_pairs={{1,0},{2,1},{3,2},{4,3},{5,4},{6,5},{7,6},{8,7},{9,8},{10,9},{11,1... | collective-permute-start | bytes 6291464 | tf_op jit(solution)/shard_map/ppermute | solution.py:20
  79.5 206.9 %slice-start.2 = ((bf16[1024,1536]{1,0:T(8,128)(2,1)}), bf16[1024,512]{1,0:T(8,128)(2,1)S(1)}, s32[]{:S(2)}) async-start(bf16[1024,1536]{1,0:T(8,128)(2,1)} %copy-done.3), calls=%async_computation.3 | async-start | bytes 2097152 | tf_op jit(solution)/shard_map/slice | solution.py:61
  286.4 146.5 %copy-start.8 = (f32[512]{0:T(512)S(1)}, f32[512]{0:T(512)}, u32[]{:S(2)}) copy-start(f32[512]{0:T(512)} %param.14) | copy-start | bytes 6148
  286.5 1.0 copy-start.4
  297.9 3.5 slice-start
  298.4 2.5 copy-start.2
  298.4 3.3 slice-start.1
  321.4 1.2 copy-start.5
  334.0 3.5 slice-start
  334.6 2.5 copy-start.2
  334.6 3.3 slice-start.1
  357.6 1.2 copy-start.5
  370.2 3.5 slice-start
  370.8 2.5 copy-start.2
  370.8 3.3 slice-start.1
  393.8 1.2 copy-start.5
  395.0 1.0 copy-start.4
  406.4 3.5 slice-start
  407.0 2.5 copy-start.2
  407.0 3.3 slice-start.1
  430.0 1.2 copy-start.5
  431.2 3.2 copy-start.9
  431.2 4.9 %copy-start.1 = (bf16[512,1536]{1,0:T(8,128)(2,1)S(1)}, bf16[512,1536]{1,0:T(8,128)(2,1)}, u32[]{:S(2)}) copy-start(bf16[512,1536]{1,0:T(8,128)(2,1)} %param.13) | copy-start | bytes 4718596
  (2 other events, 2.0 us)
Sparse Core Ops, SparseCore 0:
  16.4 261.0 all-gather.3
where the time goes:
time: 444 us; the launch traced here: 443 us
  waiting for transfers between devices  237 us (53%)
  matrix products  85.5 us (19%)
  local copies, waits for them, and re-layouts  62.4 us (14%)
  other arithmetic  32 us (7%)
  between operations  13.5 us (3%)
  starting transfers between devices  11.7 us (3%)
    all_gather x1, waiting for transfers between devices, per_device(): lax.all_gather(key_value[local_src], ('region', 'sub'), axis=0, tiled=True)  198 us
    ppermute x4, waiting for transfers between devices, passed_along(): return lax.ppermute(block, axis, route)  38.9 us
    dot_general x32, matrix products, one_group(): jnp.einsum('gqk,kc->gqc', coarse_weights, coarse_values, preferred_elemen...  28.4 us
    gather x4, local copies, waits for them, and re-layouts, one_group(): fine_kv = window[slots].reshape(group_size, NADJ * BLOCK, 2 * D)  26.7 us
    dot_general x32, matrix products, one_group(): jnp.einsum('gqc,kc->gqk', head_query, coarse_keys, preferred_element_type...  24.7 us
    unnamed x23, local copies, waits for them, and re-layouts  20.3 us
    dot_general x32, matrix products, one_group(): jnp.einsum('gqc,gkc->gqk', head_query, fine_keys, preferred_element_type=...  17.4 us
    reduce_sum x32, other arithmetic, one_group(): jnp.sum(coarse_exp, axis=-1, keepdims=True)  16.2 us
  transfers between devices with their start and end apart: 5, of which 3 were waited for; matrix products, arithmetic and copies ran while one was open for 3% of the time, Pallas kernels for 0%

commit v1 on v0

v1 whole, which is shorter than its diff:
```python
import functools

import jax
import jax.numpy as jnp
from jax import lax
from jax.experimental import pallas as pl
from jax.experimental.pallas import tpu as pltpu
from jax.sharding import PartitionSpec as P

D = 512
HEADS = 8
HW = D // HEADS
BLOCK = 64
NADJ = 7
BLK = 16
ROWS = BLK * BLOCK
CN = 20
CBLK = 40
WIN = 5 * BLK
NB = WIN + CBLK
CHUNK = 256
NCH = ROWS // CHUNK
CPAD = 48
GRP = 4
LOG_CAP = 60.0
BF = jnp.bfloat16
F32 = jnp.float32
I32 = jnp.int32
MESH = pl.DeviceIdType.MESH
NT = (((1,), (1,)), ((), ()))
neg_large = -1e30


def rms(vals, gain):
    mean_square = jnp.mean(vals * vals, axis=-1, keepdims=True)
    return (vals * lax.rsqrt(mean_square + 1e-06) * gain).astype(BF)


def place(x, y, z, c):
    return (lax.rem(z, 2) * 4 + y, (z // 2) * 8 + x * 2 + c)


def gather_kernel(
    feats, gain, w, src, adj, fine, mask,
    q_out, kv_out, list_out, stat_out,
    normed, nbr, picked, half, ag, kv, q_buf, lists, stats,
    send_n, recv_n, relay_send, a_sem, b_send, b_recv, c_send, c_recv, d_send, d_recv, e_send, e_recv,
    out_sem, misc_sem,
):
    r = lax.axis_index("region")
    s = lax.axis_index("sub")
    z_lo, y = r // 4, lax.rem(r, 4)
    z_hi, x, c = s // 8, lax.rem(s // 2, 4), lax.rem(s, 2)
    z = z_hi * 2 + z_lo
    me = r * 16 + s
    has = [r > 0, r < 7, s > 0, s < 15]
    partner = (r, s + 1 - 2 * c)
    y_next, y_prev, y_far = (place(x, lax.rem(y + k, 4), z, c) for k in (1, 3, 2))
    z_next, z_prev = (place(x, y, lax.rem(z + k, 4), c) for k in (1, 3))
    x_next, x_prev = (place(lax.rem(x + k, 4), y, z, c) for k in (1, 3))
    nbr_dev = [(r - 1, s), (r + 1, s), (r, s - 1), (r, s + 1)]

    for d in range(4):

        @pl.when(jnp.logical_not(has[d]))
        def _():
            nbr[d] = jnp.zeros((ROWS, D), BF)

    barrier = pltpu.get_barrier_semaphore()
    for dev in (partner, y_next, y_prev, y_far, z_next, z_prev, x_next, x_prev):
        pl.semaphore_signal(barrier, inc=1, device_id=dev, device_id_type=MESH)
    for d in range(4):

        @pl.when(has[d])
        def _():
            pl.semaphore_signal(barrier, inc=1, device_id=nbr_dev[d], device_id_type=MESH)

    src_row = (src[...] - me * ROWS).astype(F32)
    rows32 = lax.broadcasted_iota(I32, (32, CN), 0)
    cols32 = lax.broadcasted_iota(I32, (32, CN), 1)
    src_col = jnp.sum(jnp.where(rows32 == cols32, src_row, 0.0), axis=1, keepdims=True).astype(I32)
    hot = (lax.broadcasted_iota(I32, (32, ROWS), 1) == src_col).astype(BF)
    mine = rms(jnp.dot(hot, feats[...], preferred_element_type=F32), gain[...])
    picked[0] = mine[:, : D // 2]
    picked[1] = mine[:, D // 2 :]

    n_near = 8 + sum(h.astype(I32) for h in has)
    pl.semaphore_wait(barrier, n_near)

    def copy(src_ref, dst_ref, ss, rs, dev):
        return pltpu.make_async_remote_copy(
            src_ref=src_ref, dst_ref=dst_ref, send_sem=ss, recv_sem=rs, device_id=dev, device_id_type=MESH
        )

    a_copy = copy(picked.at[1 - c], half, a_sem.at[0], a_sem.at[1], partner)
    a_copy.start()

    def send_side(d, ch, dev, slot=None):
        slot = d ^ 1 if slot is None else slot
        rows = pl.ds(pl.multiple_of(ch * CHUNK, CHUNK), CHUNK)
        return copy(normed.at[rows], nbr.at[slot, rows], send_n.at[d, ch], recv_n.at[slot, ch], dev)

    def relay_side(d, ch, dev):
        rows = pl.ds(pl.multiple_of(ch * CHUNK, CHUNK), CHUNK)
        return copy(nbr.at[d, rows], nbr.at[d ^ 1, rows], relay_send.at[ch - 2], recv_n.at[d ^ 1, ch], dev)

    def side_to(d, ch):
        if d >= 2:
            return nbr_dev[d], d ^ 1
        turn = ((r == 4) if d == 0 else (r == 3)) & (ch >= 2)
        far = 0 if d == 0 else 7
        return (jnp.where(turn, far, nbr_dev[d][0]), s), jnp.where(turn, d, d ^ 1)

    def start_sides(dirs, ch):
        for d in dirs:

            @pl.when(has[d])
            def _():
                send_side(d, ch, *side_to(d, ch)).start()

    def norm_chunk(i, carry):
        ch = lax.rem(i + 2, NCH)
        rows = pl.ds(pl.multiple_of(ch * CHUNK, CHUNK), CHUNK)
        normed[rows] = rms(feats[rows].astype(F32), gain[...])
        start_sides((0, 1), ch)
        return carry

    lax.fori_loop(0, NCH, norm_chunk, 0)

    a_copy.wait()
    r48 = lax.broadcasted_iota(I32, (CPAD, 64), 0)
    c48 = lax.broadcasted_iota(I32, (CPAD, 64), 1)
    first = r48 < CN
    pick = jnp.where(first, r48, r48 + 12) == c48
    pick = (pick & (r48 < 2 * CN)).astype(BF)
    own_half = picked[c]
    lo = jnp.where(c == 0, own_half, half[...])
    hi = jnp.where(c == 0, half[...], own_half)
    ag[c, x, z, y] = jnp.dot(pick, jnp.concatenate([lo, hi], axis=0), preferred_element_type=F32).astype(BF)

    blk_ref = ag.at[c, x, z, y]
    b_copies = [copy(blk_ref, blk_ref, b_send.at[i], b_recv.at[i], dev) for i, dev in enumerate((y_next, y_prev, y_far))]
    for b in b_copies:
        b.start()

    heads_of = (lax.broadcasted_iota(I32, (D, 128), 0) // HW == lax.broadcasted_iota(I32, (D, 128), 1)).astype(BF)
    stats[...] = jnp.zeros_like(stats)

    def top_norm(vals):
        sq = (vals.astype(F32) * vals.astype(F32)).astype(BF)
        sums = jnp.dot(sq, heads_of, preferred_element_type=F32)
        return jnp.max(sums, axis=0, keepdims=True)

    def put_kv(vals, block, count, sem):
        kv[pl.ds(block, count)] = vals.reshape(count, BLOCK, 2 * D)
        stats[0:1] = jnp.maximum(stats[0:1], top_norm(vals[:, :D]))
        pltpu.make_async_copy(kv.at[pl.ds(block, count)], kv_out.at[pl.ds(block, count)], out_sem.at[sem]).start()

    def own_chunk(ch):
        rows = slice(ch * CHUNK, (ch + 1) * CHUNK)
        vals = normed[rows]
        qv = jnp.dot(vals, w[:, :D], preferred_element_type=F32).astype(BF) * jnp.asarray(HW**-0.5, BF)
        q_buf[rows] = qv
        stats[1:2] = jnp.maximum(stats[1:2], top_norm(qv))
        kvv = jnp.dot(vals, w[:, D:], preferred_element_type=F32).astype(BF)
        put_kv(kvv, 4 * ch, 4, ch)

    own_chunk(0)
    for b in b_copies:
        b.wait()

    def ring(slab, at, nxt, prv, snd, rcv, early, late):
        prev_at, next_at, far_at = (lax.rem(at + k, 4) for k in (3, 1, 2))
        to_next = [copy(slab(at, h), slab(at, h), snd.at[0, h], rcv.at[0, h], nxt) for h in range(2)]
        to_prev = [copy(slab(at, h), slab(at, h), snd.at[1, h], rcv.at[1, h], prv) for h in range(2)]
        for a in (to_next[0], to_prev[1], to_next[1], to_prev[0]):
            a.start()
        early()
        to_next[0].wait_recv()
        on_next = copy(slab(prev_at, 0), slab(prev_at, 0), snd.at[2, 0], rcv.at[2, 0], nxt)
        on_next.start()
        to_prev[1].wait_recv()
        on_prev = copy(slab(next_at, 1), slab(next_at, 1), snd.at[2, 1], rcv.at[2, 1], prv)
        on_prev.start()
        to_next[1].wait_recv()
        to_prev[0].wait_recv()
        late(prev_at, next_at)
        on_next.wait_recv()
        on_prev.wait_recv()
        for a in to_next + to_prev + [on_next, on_prev]:
            a.wait_send()
        return far_at

    ring(
        lambda i, h: ag.at[c, x, i, pl.ds(2 * h, 2)], z, z_next, z_prev, c_send, c_recv,
        lambda: own_chunk(1), lambda p, n: None,
    )

    def e_copy(i):
        return copy(ag.at[c, i], ag.at[c, i], e_send.at[i], e_recv.at[i], partner)

    def e_start(i):
        e_copy(i).start()

    def d_early():
        e_start(x)

        def sides(i, carry):
            start_sides((2, 3), lax.rem(i + 2, NCH))
            return carry

        lax.fori_loop(0, NCH, sides, 0)
        own_chunk(2)
        own_chunk(3)
        q_copy = pltpu.make_async_copy(q_buf, q_out, misc_sem.at[0])
        q_copy.start()
        dev_of, local = adj[...] // BLK, lax.rem(adj[...], BLK)
        gap = dev_of - me
        side = jnp.where(gap == -16, 1, jnp.where(gap == 16, 2, jnp.where(gap == -1, 3, jnp.where(gap == 1, 4, 0))))
        slot = side * BLK + local
        fine_live = (fine[...] == 1) | (lax.broadcasted_iota(I32, (BLK, NADJ), 1) == 0)
        fine_n = fine_live.astype(I32)
        coarse_n = (mask[...] == 1).astype(I32)
        spot = lax.broadcasted_iota(I32, (BLK, 128), 1)
        found = jnp.full((BLK, 128), NB, I32)
        count = jnp.zeros((BLK, 1), I32)
        for j in range(CBLK):
            live = coarse_n[:, j : j + 1]
            found = jnp.where(spot == jnp.where(live == 1, count, -1), WIN + j, found)
            count = count + live
        for j in range(NADJ):
            live = fine_n[:, j : j + 1]
            found = jnp.where(spot == jnp.where(live == 1, count, -1), slot[:, j : j + 1], found)
            count = count + live
        lists[...] = jnp.where(spot == 127, count, found)
        pltpu.make_async_copy(lists, list_out, misc_sem.at[1]).start()

    def d_late(p, n):
        e_start(p)
        e_start(n)
        relay = [(7, 1, 4), (0, 0, 3)]
        for at, d, to in relay:

            @pl.when(r == at)
            def _():
                for ch in (2, 3):
                    side = send_side(d ^ 1, ch, (to, s))
                    side.wait_recv()
                    relay_side(d, ch, (to, s)).start()

    far = ring(
        lambda i, h: ag.at[c, i, pl.ds(2 * h, 2)], x, x_next, x_prev, d_send, d_recv, d_early, d_late
    )
    e_start(far)

    def e_wait(i, carry):
        e_copy(i).wait()
        return carry

    lax.fori_loop(0, 4, e_wait, 0)

    r160 = lax.broadcasted_iota(I32, (160, 4 * CPAD), 0)
    c160 = lax.broadcasted_iota(I32, (160, 4 * CPAD), 1)
    sel = ((r160 // 40) * CPAD + lax.rem(r160, 40) == c160).astype(BF)

    def coarse_part(i, carry):
        zl, yy = i // 4, lax.rem(i, 4)
        parts = []
        for zh in range(2):
            zz = zh * 2 + zl
            cols = []
            for h in range(2):
                got = jnp.concatenate([ag[h, k, zz, yy] for k in range(4)], axis=0)
                cols.append(jnp.dot(sel, got, preferred_element_type=F32).astype(BF))
            parts.append(jnp.concatenate(cols, axis=1))
        vals = jnp.concatenate(parts, axis=0)
        put_kv(jnp.dot(vals, w[:, D:], preferred_element_type=F32).astype(BF), WIN + 5 * i, 5, 20 + i)
        return carry

    lax.fori_loop(0, 8, coarse_part, 0)

    def side_part(i, carry):
        ch = lax.rem(i + 2, NCH)
        for d in (2, 3, 0, 1):

            @pl.when(has[d])
            def _():
                send_side(d ^ 1, ch, nbr_dev[d]).wait_recv()

            rows = pl.ds(pl.multiple_of(ch * CHUNK, CHUNK), CHUNK)
            vals = jnp.dot(nbr[d, rows], w[:, D:], preferred_element_type=F32).astype(BF)
            put_kv(vals, (d + 1) * BLK + 4 * ch, 4, 4 + d * 4 + ch)
        return carry

    lax.fori_loop(0, NCH, side_part, 0)

    stat_copy = pltpu.make_async_copy(stats, stat_out, misc_sem.at[2])
    stat_copy.start()

    def send_wait(ch, carry):
        for d in range(4):

            @pl.when(has[d])
            def _():
                send_side(d, ch, nbr_dev[d]).wait_send()

        return carry

    lax.fori_loop(0, NCH, send_wait, 0)
    for at, d, to in ((7, 1, 4), (0, 0, 3)):

        @pl.when(r == at)
        def _():
            for ch in (2, 3):
                relay_side(d, ch, (to, s)).wait_send()

    def out_wait(i, carry):
        pltpu.make_async_copy(kv.at[pl.ds(4 * i, 4)], kv_out.at[pl.ds(4 * i, 4)], out_sem.at[i]).wait()
        return carry

    def out_wait_c(i, carry):
        at = pl.ds(WIN + 5 * i, 5)
        pltpu.make_async_copy(kv.at[at], kv_out.at[at], out_sem.at[20 + i]).wait()
        return carry

    lax.fori_loop(0, 20, out_wait, 0)
    lax.fori_loop(0, 8, out_wait_c, 0)
    pltpu.make_async_copy(q_buf, q_out, misc_sem.at[0]).wait()
    pltpu.make_async_copy(lists, list_out, misc_sem.at[1]).wait()
    stat_copy.wait()


def attend_kernel(unroll, lists, q_hbm, kv_hbm, stats, gain, w, out, q, kv, qm, acc, lsum, sems):
    q_copy = pltpu.make_async_copy(q_hbm, q, sems.at[0])
    kv_copy = pltpu.make_async_copy(kv_hbm, kv.at[pl.ds(0, NB)], sems.at[1])
    q_copy.start()
    kv_copy.start()
    lane = lax.broadcasted_iota(I32, (BLOCK, 256), 1) // HW
    zero = jnp.zeros((), BF)
    acc[...] = jnp.zeros_like(acc)
    lsum[...] = jnp.zeros_like(lsum)
    kv[NB] = jnp.zeros((BLOCK, 2 * D), BF)
    qm[BLK] = jnp.zeros((2, 256, 256), BF)
    q_copy.wait()

    def spread(b, carry):
        rows = pl.ds(pl.multiple_of(b * BLOCK, BLOCK), BLOCK)
        for g in range(2):
            qb = q[rows, g * 256 : (g + 1) * 256]
            for h in range(4):
                qm[b, g, h * BLOCK : (h + 1) * BLOCK, :] = jnp.where(lane == h, qb, zero)
        return carry

    lax.fori_loop(0, BLK, spread, 0)
    kv_copy.wait()

    bound = jnp.max(jnp.sqrt(stats[0:1]) * jnp.sqrt(stats[1:2])) * 1.02
    safe = bound < LOG_CAP

    def groups(b):
        return jnp.where(b < BLK, (lists[jnp.minimum(b, BLK - 1), 127] + GRP - 1) // GRP, 0)

    def blocks_of(b, t, lo):
        bb = jnp.minimum(b, BLK - 1)
        return jnp.concatenate([kv[lists[bb, t * GRP + j], :, lo : lo + 256] for j in range(GRP)], axis=0)

    def scores(b, t, g):
        return lax.dot_general(qm[b, g], blocks_of(b, t, g * 256), NT, preferred_element_type=F32)

    key_lane = lax.broadcasted_iota(I32, (1, 256), 1)

    def open_keys(b, t):
        bb = jnp.minimum(b, BLK - 1)
        return key_lane < (lists[bb, 127] - t * GRP) * BLOCK

    def add_up(b, t, g, p, keys):
        kept = jnp.where(keys, p, 0.0)
        lsum[b, g] += kept[:, :128] + kept[:, 128:]
        acc[b, g] += jnp.dot(p.astype(BF), blocks_of(b, t, D + g * 256), preferred_element_type=F32)

    @pl.when(safe)
    def _():
        total = functools.reduce(lambda a, b: a + b, [groups(b) for b in range(BLK)])

        def step_on(b, t):
            last = t + 1 >= groups(b)
            return jnp.where(last, jnp.minimum(b + 1, BLK), b), jnp.where(last, 0, t + 1)

        def body(i, at):
            spots = [at]
            for _ in range(unroll):
                spots.append(step_on(*spots[-1]))
            held = [scores(*spots[0], g) for g in range(2)]
            for u in range(unroll):
                later = [scores(*spots[u + 1], g) for g in range(2)] if u + 1 < unroll else None
                keys = open_keys(*spots[u])
                for g in range(2):
                    add_up(*spots[u], g, jnp.exp(held[g]), keys)
                held = later
            return spots[-1]

        lax.fori_loop(0, (total + unroll - 1) // unroll, body, (jnp.int32(0), jnp.int32(0)))

    @pl.when(jnp.logical_not(safe))
    def _():
        def block(b, carry):
            for g in range(2):
                def peak(t, m):
                    sc = jnp.where(open_keys(b, t), scores(b, t, g), neg_large)
                    return jnp.maximum(m, jnp.max(sc, axis=-1, keepdims=True))

                top = lax.fori_loop(0, groups(b), peak, jnp.full((256, 1), neg_large, F32))

                def weigh(t, carry):
                    keys = open_keys(b, t)
                    sc = jnp.where(keys, scores(b, t, g), neg_large)
                    add_up(b, t, g, jnp.exp(sc - top), keys)
                    return carry

                lax.fori_loop(0, groups(b), weigh, 0)
            return carry

        lax.fori_loop(0, BLK, block, 0)

    def finish(b, carry):
        pieces = []
        for g in range(2):
            piece = jnp.zeros((BLOCK, 256), F32)
            for h in range(4):
                rows = slice(h * BLOCK, (h + 1) * BLOCK)
                total = jnp.sum(lsum[b, g, rows, :], axis=-1, keepdims=True)
                piece = jnp.where(lane == h, acc[b, g, rows, :] / total, piece)
            pieces.append(piece)
        attended = jnp.concatenate(pieces, axis=1).astype(BF).astype(F32)
        rows = pl.ds(pl.multiple_of(b * BLOCK, BLOCK), BLOCK)
        q[rows] = rms(attended, gain[...])
        return carry

    lax.fori_loop(0, BLK, finish, 0)
    for i in range(4):
        rows = slice(i * CHUNK, (i + 1) * CHUNK)
        out[rows] = jnp.dot(q[rows], w[...], preferred_element_type=F32).astype(BF)


def per_device(node_feats, gain_in, w_qkv, gain_out, w_out, adjacency, fine_valid, coarse_mask, coarse_src):
    vmem = pl.BlockSpec(memory_space=pltpu.VMEM)
    anywhere = pl.BlockSpec(memory_space=pl.ANY)
    dma = pltpu.SemaphoreType.DMA
    q, kv, lists, stats = pl.pallas_call(
        gather_kernel,
        out_shape=(
            jax.ShapeDtypeStruct((ROWS, D), BF),
            jax.ShapeDtypeStruct((NB, BLOCK, 2 * D), BF),
            jax.ShapeDtypeStruct((BLK, 128), I32),
            jax.ShapeDtypeStruct((8, 128), F32),
        ),
        in_specs=[vmem] * 7,
        out_specs=(anywhere,) * 4,
        scratch_shapes=[
            pltpu.VMEM((ROWS, D), BF),
            pltpu.VMEM((4, ROWS, D), BF),
            pltpu.VMEM((2, 32, D // 2), BF),
            pltpu.VMEM((32, D // 2), BF),
            pltpu.VMEM((2, 4, 4, 4, CPAD, D // 2), BF),
            pltpu.VMEM((NB, BLOCK, 2 * D), BF),
            pltpu.VMEM((ROWS, D), BF),
            pltpu.VMEM((BLK, 128), I32),
            pltpu.VMEM((8, 128), F32),
            dma((4, 4)), dma((4, 4)), dma((2,)), dma((2,)), dma((3,)), dma((3,)),
            dma((3, 2)), dma((3, 2)), dma((3, 2)), dma((3, 2)), dma((4,)), dma((4,)),
            dma((28,)), dma((3,)),
        ],
        compiler_params=pltpu.CompilerParams(
            collective_id=0, has_side_effects=True, vmem_limit_bytes=48 * 2**20
        ),
    )(
        node_feats, gain_in.reshape(1, D), w_qkv, coarse_src.reshape(1, CN),
        adjacency, fine_valid, coarse_mask,
    )
    smem = pl.BlockSpec(memory_space=pltpu.SMEM)
    return pl.pallas_call(
        functools.partial(attend_kernel, 8),
        out_shape=jax.ShapeDtypeStruct((ROWS, D), BF),
        in_specs=[smem, anywhere, anywhere, vmem, vmem, vmem],
        out_specs=vmem,
        scratch_shapes=[
            pltpu.VMEM((ROWS, D), BF),
            pltpu.VMEM((NB + 1, BLOCK, 2 * D), BF),
            pltpu.VMEM((BLK + 1, 2, 256, 256), BF),
            pltpu.VMEM((BLK + 1, 2, 256, 256), F32),
            pltpu.VMEM((BLK + 1, 2, 256, 128), F32),
            dma((2,)),
        ],
        compiler_params=pltpu.CompilerParams(vmem_limit_bytes=56 * 2**20),
    )(lists, q, kv, stats, gain_out.reshape(1, D), w_out)


def solution(mesh):
    both = ("region", "sub")
    in_specs = (P(both, None), P(), P(), P(), P(), P(both, None), P(both, None), P(both, None), P(both))
    return jax.shard_map(per_device, mesh=mesh, in_specs=in_specs, out_specs=P(both, None), check_vma=False)
```

time: 444 us -> 258 us (0.58)
  Pallas kernels: 0 us -> 247 us
  waiting for transfers between devices: 237 us -> 0 us
  matrix products: 85.5 us -> 0 us
  local copies, waits for them, and re-layouts: 62.4 us -> 8.34 us
  other arithmetic: 32 us -> 0 us
  between operations: 13.5 us -> 0.03 us
  starting transfers between devices: 11.7 us -> 0 us
    pallas_call x0 -> x2, Pallas kernels: none -> 247 us  [the longest x1 168 us: per_device(): pl.pallas_call(functools.partial(attend_kernel, 8), out_shape=jax.ShapeDt...]
    all_gather x1 -> x0, waiting for transfers between devices: 198 us -> none  [per_device(): lax.all_gather(key_value[local_src], ('region', 'sub'), axis=0, tiled=True)]
    dot_general x130 -> x0, matrix products: 85.5 us -> none  [the longest x32 28.4 us: one_group(): jnp.einsum('gqk,kc->gqc', coarse_weights, coarse_values, preferred_elemen...]
    ppermute x4 -> x0, waiting for transfers between devices: 38.9 us -> none  [passed_along(): return lax.ppermute(block, axis, route)]
    gather x5 -> x0, local copies, waits for them, and re-layouts: 27.9 us -> none  [the longest x4 26.7 us: one_group(): fine_kv = window[slots].reshape(group_size, NADJ * BLOCK, 2 * D)]
    reduce_sum x66 -> x0, other arithmetic: 26.8 us -> none  [the longest x32 16.2 us: one_group(): jnp.sum(coarse_exp, axis=-1, keepdims=True)]
    unnamed x23 -> x18, local copies, waits for them, and re-layouts: 20.3 us -> 8.34 us
    ppermute x4 -> x0, starting transfers between devices: 11.7 us -> none  [passed_along(): return lax.ppermute(block, axis, route)]
  transfers between devices with their start and end apart: 5 -> 0, of which waited for: 3 -> 0; matrix products, arithmetic and copies ran while one was open for 3% -> 0% of each run, Pallas kernels for 0% -> 0%
where the time goes in v1:
time: 258 us; the launch traced here: 256 us
  Pallas kernels  247 us (96%)
  local copies, waits for them, and re-layouts  8.34 us (3%)
    pallas_call x1, Pallas kernels, per_device(): pl.pallas_call(functools.partial(attend_kernel, 8), out_shape=jax.ShapeDt...  168 us
    pallas_call x1, Pallas kernels, per_device(): pl.pallas_call(gather_kernel, out_shape=(jax.ShapeDtypeStruct((ROWS, D),...  78.9 us
    unnamed x18, local copies, waits for them, and re-layouts  8.34 us

profile of v1, /device:TPU:2, one launch (start us, length us, event | category | flops | bytes accessed | tf_op | source)
XLA Modules:
  0.0 255.8 jit_solution(13119042244934575048)
XLA Ops:
  0.0 0.8 copy.10.adj
  0.8 0.8 copy.11.fine
  1.5 0.0 copy-start
  1.5 1.4 copy-done
  2.9 0.0 copy-start.2
  2.9 1.2 copy-done.2
  4.2 0.0 copy-start.4
  4.2 0.7 copy-done.4
  4.9 0.0 copy-start.6
  4.9 0.7 copy-done.6
  5.5 0.0 copy-start.7
  5.5 0.7 copy-done.7
  6.2 78.9 %shard_map.91 = (bf16[1024,512]{1,0:T(8,128)(2,1)S(1)}, bf16[120,64,1024]{2,1,0:T(8,128)(2,1)}, s32[16,128]{1,0:T(8,128)S(1)}, f32[8,128]{1,0:T(8,128)S(1)}) custom-call(bf16[1024,512]{1,0:T(8,128)(2,1)S(1)} %copy-done.2, f32[1,512]{1,0:T(1,128)S(1)} %bitcast.3, bf16[512,1536]{1,0:T(8,128)(2,1)S(1)} %copy-done, s32[1,20]{1,0:T(1,128)S(1)} %bitcast.4, ...), custom_call_target="tpu_custom_call" | custom-call | tf_op jit(solution)/shard_map/pallas_call | solution.py:449
  85.1 0.0 copy-start.1
  85.2 1.0 copy-done.1
  86.1 0.0 copy-start.3
  86.1 0.6 copy-done.3
  86.7 0.0 copy-start.5
  86.7 0.6 copy-done.5
  87.3 168.5 %shard_map.92 = bf16[1024,512]{1,0:T(8,128)(2,1)} custom-call(s32[16,128]{1,0:T(8,128)} %copy-done.3, bf16[1024,512]{1,0:T(8,128)(2,1)} %copy-done.1, bf16[120,64,1024]{2,1,0:T(8,128)(2,1)} %get-tuple-element.11.kv_hbm, f32[8,128]{1,0:T(8,128)} %copy-done.5, f32[1,512]{1,0:T(1,128)} %bitcast.5, bf16[512,512]{1,0:T(8,128)(2,1)} %w.3), custom_call_target="tpu_custom_call" | custom-call | tf_op jit(solution)/shard_map/pallas_call | solution.py:481
Async XLA Ops:
  1.5 1.4 copy-start
  2.9 1.2 copy-start.2
  4.2 0.7 copy-start.4
  4.9 0.7 copy-start.6
  5.5 0.7 copy-start.7
  85.1 1.0 copy-start.1
  86.1 0.6 copy-start.3
  86.7 0.6 copy-start.5

commit v2 on v1

--- a/solution.py
+++ b/solution.py
@@ -23,6 +23,8 @@
 CPAD = 48
 GRP = 4
 LOG_CAP = 60.0
+EARLY_X = ()
+LATE_X = (2, 3, 0, 1)
 BF = jnp.bfloat16
 F32 = jnp.float32
 I32 = jnp.int32
@@ -41,11 +43,10 @@
 
 
 def gather_kernel(
-    feats, gain, w, src, adj, fine, mask,
-    q_out, kv_out, list_out, stat_out,
-    normed, nbr, picked, half, ag, kv, q_buf, lists, stats,
-    send_n, recv_n, relay_send, a_sem, b_send, b_recv, c_send, c_recv, d_send, d_recv, e_send, e_recv,
-    out_sem, misc_sem,
+    feats_hbm, gain_hbm, w_hbm, src_hbm, adj_hbm, fine_hbm, mask_hbm,
+    qm, kv, lists, stats,
+    feats, gain, w, src, adj, fine, mask, normed, nbr, picked, half, ag,
+    send_n, recv_n, relay_send, a_sem, b_send, b_recv, c_send, c_recv, d_send, d_recv, e_send, e_recv, in_sem,
 ):
     r = lax.axis_index("region")
     s = lax.axis_index("sub")
@@ -60,6 +61,15 @@
     x_next, x_prev = (place(lax.rem(x + k, 4), y, z, c) for k in (1, 3))
     nbr_dev = [(r - 1, s), (r + 1, s), (r, s - 1), (r, s + 1)]
 
+    loads = [
+        pltpu.make_async_copy(a, b, in_sem.at[i])
+        for i, (a, b) in enumerate(
+            ((src_hbm, src), (gain_hbm, gain), (feats_hbm, feats), (w_hbm, w), (adj_hbm, adj), (fine_hbm, fine), (mask_hbm, mask))
+        )
+    ]
+    for load in loads:
+        load.start()
+
     for d in range(4):
 
         @pl.when(jnp.logical_not(has[d]))
@@ -75,6 +85,8 @@
         def _():
             pl.semaphore_signal(barrier, inc=1, device_id=nbr_dev[d], device_id_type=MESH)
 
+    for load in loads[:3]:
+        load.wait()
     src_row = (src[...] - me * ROWS).astype(F32)
     rows32 = lax.broadcasted_iota(I32, (32, CN), 0)
     cols32 = lax.broadcasted_iota(I32, (32, CN), 1)
@@ -111,22 +123,22 @@
         far = 0 if d == 0 else 7
         return (jnp.where(turn, far, nbr_dev[d][0]), s), jnp.where(turn, d, d ^ 1)
 
-    def start_sides(dirs, ch):
+    def start_sides(dirs, ch, crossing=None):
         for d in dirs:
-
-            @pl.when(has[d])
+            now = has[d]
+            if crossing is not None:
+                over = (r == 4) if d == 0 else (r == 3)
+                now = now & (over if crossing else jnp.logical_not(over))
+
+            @pl.when(now)
             def _():
                 send_side(d, ch, *side_to(d, ch)).start()
 
-    def norm_chunk(i, carry):
-        ch = lax.rem(i + 2, NCH)
-        rows = pl.ds(pl.multiple_of(ch * CHUNK, CHUNK), CHUNK)
+    def norm_chunk(ch):
+        rows = pl.ds(ch * CHUNK, CHUNK)
         normed[rows] = rms(feats[rows].astype(F32), gain[...])
-        start_sides((0, 1), ch)
-        return carry
-
-    lax.fori_loop(0, NCH, norm_chunk, 0)
-
+
+    norm_chunk(2)
     a_copy.wait()
     r48 = lax.broadcasted_iota(I32, (CPAD, 64), 0)
     c48 = lax.broadcasted_iota(I32, (CPAD, 64), 1)
@@ -142,6 +154,10 @@
     b_copies = [copy(blk_ref, blk_ref, b_send.at[i], b_recv.at[i], dev) for i, dev in enumerate((y_next, y_prev, y_far))]
     for b in b_copies:
         b.start()
+    for ch in (3, 0, 1):
+        norm_chunk(ch)
+    for load in loads[3:]:
+        load.wait()
 
     heads_of = (lax.broadcasted_iota(I32, (D, 128), 0) // HW == lax.broadcasted_iota(I32, (D, 128), 1)).astype(BF)
     stats[...] = jnp.zeros_like(stats)
@@ -151,23 +167,35 @@
         sums = jnp.dot(sq, heads_of, preferred_element_type=F32)
         return jnp.max(sums, axis=0, keepdims=True)
 
-    def put_kv(vals, block, count, sem):
+    def put_kv(vals, block, count):
         kv[pl.ds(block, count)] = vals.reshape(count, BLOCK, 2 * D)
         stats[0:1] = jnp.maximum(stats[0:1], top_norm(vals[:, :D]))
-        pltpu.make_async_copy(kv.at[pl.ds(block, count)], kv_out.at[pl.ds(block, count)], out_sem.at[sem]).start()
+
+    lane_head = lax.broadcasted_iota(I32, (CHUNK, 256), 1) // HW
 
     def own_chunk(ch):
-        rows = slice(ch * CHUNK, (ch + 1) * CHUNK)
-        vals = normed[rows]
+        vals = normed[pl.ds(ch * CHUNK, CHUNK)]
         qv = jnp.dot(vals, w[:, :D], preferred_element_type=F32).astype(BF) * jnp.asarray(HW**-0.5, BF)
-        q_buf[rows] = qv
         stats[1:2] = jnp.maximum(stats[1:2], top_norm(qv))
-        kvv = jnp.dot(vals, w[:, D:], preferred_element_type=F32).astype(BF)
-        put_kv(kvv, 4 * ch, 4, ch)
-
-    own_chunk(0)
+        for g in range(2):
+            for h in range(4):
+                qh = jnp.where(lane_head == h, qv[:, g * 256 : (g + 1) * 256], jnp.zeros((), BF))
+                qm[pl.ds(4 * ch, 4), g, h * BLOCK : (h + 1) * BLOCK, :] = qh.reshape(4, BLOCK, 256)
+        put_kv(jnp.dot(vals, w[:, D:], preferred_element_type=F32).astype(BF), 4 * ch, 4)
+
     for b in b_copies:
         b.wait()
+
+    def side_part(ch, dirs):
+        for d in dirs:
+
+            @pl.when(has[d])
+            def _():
+                send_side(d ^ 1, ch, nbr_dev[d]).wait_recv()
+
+            rows = pl.ds(pl.multiple_of(ch * CHUNK, CHUNK), CHUNK)
+            vals = jnp.dot(nbr[d, rows], w[:, D:], preferred_element_type=F32).astype(BF)
+            put_kv(vals, (d + 1) * BLK + 4 * ch, 4)
 
     def ring(slab, at, nxt, prv, snd, rcv, early, late):
         prev_at, next_at, far_at = (lax.rem(at + k, 4) for k in (3, 1, 2))
@@ -191,9 +219,17 @@
             a.wait_send()
         return far_at
 
+    def c_early():
+        def sides(i, carry):
+            start_sides((0, 1), lax.rem(i + 2, NCH), False)
+            return carry
+
+        lax.fori_loop(0, NCH, sides, 0)
+        own_chunk(0)
+
     ring(
         lambda i, h: ag.at[c, x, i, pl.ds(2 * h, 2)], z, z_next, z_prev, c_send, c_recv,
-        lambda: own_chunk(1), lambda p, n: None,
+        c_early, lambda p, n: None,
     )
 
     def e_copy(i):
@@ -206,38 +242,45 @@
         e_start(x)
 
         def sides(i, carry):
-            start_sides((2, 3), lax.rem(i + 2, NCH))
+            start_sides((0, 1), lax.rem(i + 2, NCH), True)
             return carry
 
         lax.fori_loop(0, NCH, sides, 0)
+        for ch in EARLY_X:
+            start_sides((2, 3), ch)
+        own_chunk(1)
         own_chunk(2)
         own_chunk(3)
-        q_copy = pltpu.make_async_copy(q_buf, q_out, misc_sem.at[0])
-        q_copy.start()
         dev_of, local = adj[...] // BLK, lax.rem(adj[...], BLK)
         gap = dev_of - me
         side = jnp.where(gap == -16, 1, jnp.where(gap == 16, 2, jnp.where(gap == -1, 3, jnp.where(gap == 1, 4, 0))))
         slot = side * BLK + local
-        fine_live = (fine[...] == 1) | (lax.broadcasted_iota(I32, (BLK, NADJ), 1) == 0)
+        fine_live = (fine[...] == 1) | (lax.broadcasted_iota(I32, (NADJ, BLK), 0) == 0)
         fine_n = fine_live.astype(I32)
-        coarse_n = (mask[...] == 1).astype(I32)
-        spot = lax.broadcasted_iota(I32, (BLK, 128), 1)
-        found = jnp.full((BLK, 128), NB, I32)
-        count = jnp.zeros((BLK, 1), I32)
+        eye = (lax.broadcasted_iota(I32, (BLK, BLK), 0) == lax.broadcasted_iota(I32, (BLK, BLK), 1)).astype(BF)
+        coarse_n = lax.dot_general(
+            (mask[...] == 1).astype(BF), eye, (((0,), (0,)), ((), ())), preferred_element_type=F32
+        ).astype(I32)
+        spot = lax.broadcasted_iota(I32, (56, BLK), 0)
+        found = jnp.full((56, BLK), NB, I32)
+        count = jnp.zeros((1, BLK), I32)
         for j in range(CBLK):
-            live = coarse_n[:, j : j + 1]
+            live = coarse_n[j : j + 1]
             found = jnp.where(spot == jnp.where(live == 1, count, -1), WIN + j, found)
             count = count + live
         for j in range(NADJ):
-            live = fine_n[:, j : j + 1]
-            found = jnp.where(spot == jnp.where(live == 1, count, -1), slot[:, j : j + 1], found)
+            live = fine_n[j : j + 1]
+            found = jnp.where(spot == jnp.where(live == 1, count, -1), slot[j : j + 1], found)
             count = count + live
-        lists[...] = jnp.where(spot == 127, count, found)
-        pltpu.make_async_copy(lists, list_out, misc_sem.at[1]).start()
+        lists[...] = jnp.zeros_like(lists)
+        lists[:, :BLK] = jnp.where(spot == 48, count, found)
+        kv[NB] = jnp.zeros((BLOCK, 2 * D), BF)
 
     def d_late(p, n):
         e_start(p)
         e_start(n)
+        for ch in LATE_X:
+            start_sides((2, 3), ch)
         relay = [(7, 1, 4), (0, 0, 3)]
         for at, d, to in relay:
 
@@ -252,6 +295,7 @@
         lambda i, h: ag.at[c, i, pl.ds(2 * h, 2)], x, x_next, x_prev, d_send, d_recv, d_early, d_late
     )
     e_start(far)
+    side_part(2, (0, 1))
 
     def e_wait(i, carry):
         e_copy(i).wait()
@@ -274,28 +318,18 @@
                 cols.append(jnp.dot(sel, got, preferred_element_type=F32).astype(BF))
             parts.append(jnp.concatenate(cols, axis=1))
         vals = jnp.concatenate(parts, axis=0)
-        put_kv(jnp.dot(vals, w[:, D:], preferred_element_type=F32).astype(BF), WIN + 5 * i, 5, 20 + i)
+        put_kv(jnp.dot(vals, w[:, D:], preferred_element_type=F32).astype(BF), WIN + 5 * i, 5)
         return carry
 
     lax.fori_loop(0, 8, coarse_part, 0)
 
-    def side_part(i, carry):
-        ch = lax.rem(i + 2, NCH)
-        for d in (2, 3, 0, 1):
-
-            @pl.when(has[d])
-            def _():
-                send_side(d ^ 1, ch, nbr_dev[d]).wait_recv()
-
-            rows = pl.ds(pl.multiple_of(ch * CHUNK, CHUNK), CHUNK)
-            vals = jnp.dot(nbr[d, rows], w[:, D:], preferred_element_type=F32).astype(BF)
-            put_kv(vals, (d + 1) * BLK + 4 * ch, 4, 4 + d * 4 + ch)
+    side_part(2, (2, 3))
+
+    def rest(i, carry):
+        side_part(lax.rem(i + 3, NCH), (0, 1, 2, 3))
         return carry
 
-    lax.fori_loop(0, NCH, side_part, 0)
-
-    stat_copy = pltpu.make_async_copy(stats, stat_out, misc_sem.at[2])
-    stat_copy.start()
+    lax.fori_loop(0, NCH - 1, rest, 0)
 
     def send_wait(ch, carry):
         for d in range(4):
@@ -314,64 +348,38 @@
             for ch in (2, 3):
                 relay_side(d, ch, (to, s)).wait_send()
 
-    def out_wait(i, carry):
-        pltpu.make_async_copy(kv.at[pl.ds(4 * i, 4)], kv_out.at[pl.ds(4 * i, 4)], out_sem.at[i]).wait()
-        return carry
-
-    def out_wait_c(i, carry):
-        at = pl.ds(WIN + 5 * i, 5)
-        pltpu.make_async_copy(kv.at[at], kv_out.at[at], out_sem.at[20 + i]).wait()
-        return carry
-
-    lax.fori_loop(0, 20, out_wait, 0)
-    lax.fori_loop(0, 8, out_wait_c, 0)
-    pltpu.make_async_copy(q_buf, q_out, misc_sem.at[0]).wait()
-    pltpu.make_async_copy(lists, list_out, misc_sem.at[1]).wait()
-    stat_copy.wait()
-
-
-def attend_kernel(unroll, lists, q_hbm, kv_hbm, stats, gain, w, out, q, kv, qm, acc, lsum, sems):
-    q_copy = pltpu.make_async_copy(q_hbm, q, sems.at[0])
-    kv_copy = pltpu.make_async_copy(kv_hbm, kv.at[pl.ds(0, NB)], sems.at[1])
-    q_copy.start()
-    kv_copy.start()
+
+def attend_kernel(unroll, lists_vmem, qm, kv, stats, gain_hbm, w_hbm, out, lists, gain, w, mid, acc, lsum, sems):
+    loads = [
+        pltpu.make_async_copy(a, b, sems.at[i])
+        for i, (a, b) in enumerate(((lists_vmem, lists), (gain_hbm, gain), (w_hbm, w)))
+    ]
+    for load in loads:
+        load.start()
     lane = lax.broadcasted_iota(I32, (BLOCK, 256), 1) // HW
-    zero = jnp.zeros((), BF)
     acc[...] = jnp.zeros_like(acc)
     lsum[...] = jnp.zeros_like(lsum)
-    kv[NB] = jnp.zeros((BLOCK, 2 * D), BF)
-    qm[BLK] = jnp.zeros((2, 256, 256), BF)
-    q_copy.wait()
-
-    def spread(b, carry):
-        rows = pl.ds(pl.multiple_of(b * BLOCK, BLOCK), BLOCK)
-        for g in range(2):
-            qb = q[rows, g * 256 : (g + 1) * 256]
-            for h in range(4):
-                qm[b, g, h * BLOCK : (h + 1) * BLOCK, :] = jnp.where(lane == h, qb, zero)
-        return carry
-
-    lax.fori_loop(0, BLK, spread, 0)
-    kv_copy.wait()
+    for load in loads:
+        load.wait()
 
     bound = jnp.max(jnp.sqrt(stats[0:1]) * jnp.sqrt(stats[1:2])) * 1.02
     safe = bound < LOG_CAP
 
     def groups(b):
-        return jnp.where(b < BLK, (lists[jnp.minimum(b, BLK - 1), 127] + GRP - 1) // GRP, 0)
+        return jnp.where(b < BLK, (lists[48, jnp.minimum(b, BLK - 1)] + GRP - 1) // GRP, 0)
 
     def blocks_of(b, t, lo):
         bb = jnp.minimum(b, BLK - 1)
-        return jnp.concatenate([kv[lists[bb, t * GRP + j], :, lo : lo + 256] for j in range(GRP)], axis=0)
+        return jnp.concatenate([kv[lists[t * GRP + j, bb], :, lo : lo + 256] for j in range(GRP)], axis=0)
 
     def scores(b, t, g):
-        return lax.dot_general(qm[b, g], blocks_of(b, t, g * 256), NT, preferred_element_type=F32)
+        return lax.dot_general(qm[jnp.minimum(b, BLK - 1), g], blocks_of(b, t, g * 256), NT, preferred_element_type=F32)
 
     key_lane = lax.broadcasted_iota(I32, (1, 256), 1)
 
     def open_keys(b, t):
         bb = jnp.minimum(b, BLK - 1)
-        return key_lane < (lists[bb, 127] - t * GRP) * BLOCK
+        return key_lane < (lists[48, bb] - t * GRP) * BLOCK
 
     def add_up(b, t, g, p, keys):
         kept = jnp.where(keys, p, 0.0)
@@ -422,77 +430,85 @@
 
         lax.fori_loop(0, BLK, block, 0)
 
-    def finish(b, carry):
-        pieces = []
-        for g in range(2):
-            piece = jnp.zeros((BLOCK, 256), F32)
-            for h in range(4):
-                rows = slice(h * BLOCK, (h + 1) * BLOCK)
-                total = jnp.sum(lsum[b, g, rows, :], axis=-1, keepdims=True)
-                piece = jnp.where(lane == h, acc[b, g, rows, :] / total, piece)
-            pieces.append(piece)
-        attended = jnp.concatenate(pieces, axis=1).astype(BF).astype(F32)
-        rows = pl.ds(pl.multiple_of(b * BLOCK, BLOCK), BLOCK)
-        q[rows] = rms(attended, gain[...])
+    def finish(i, carry):
+        for k in range(4):
+            b = 4 * i + k
+            pieces = []
+            for g in range(2):
+                piece = jnp.zeros((BLOCK, 256), F32)
+                for h in range(4):
+                    rows = slice(h * BLOCK, (h + 1) * BLOCK)
+                    total = jnp.sum(lsum[b, g, rows, :], axis=-1, keepdims=True)
+                    piece = jnp.where(lane == h, acc[b, g, rows, :] / total, piece)
+                pieces.append(piece)
+            attended = jnp.concatenate(pieces, axis=1).astype(BF).astype(F32)
+            mid[k * BLOCK : (k + 1) * BLOCK] = rms(attended, gain[...])
+        rows = pl.ds(pl.multiple_of(i * CHUNK, CHUNK), CHUNK)
+        out[rows] = jnp.dot(mid[...], w[...], preferred_element_type=F32).astype(BF)
         return carry
 
-    lax.fori_loop(0, BLK, finish, 0)
-    for i in range(4):
-        rows = slice(i * CHUNK, (i + 1) * CHUNK)
-        out[rows] = jnp.dot(q[rows], w[...], preferred_element_type=F32).astype(BF)
+    lax.fori_loop(0, 4, finish, 0)
 
 
 def per_device(node_feats, gain_in, w_qkv, gain_out, w_out, adjacency, fine_valid, coarse_mask, coarse_src):
     vmem = pl.BlockSpec(memory_space=pltpu.VMEM)
-    anywhere = pl.BlockSpec(memory_space=pl.ANY)
+    hbm = pl.BlockSpec(memory_space=pltpu.HBM)
     dma = pltpu.SemaphoreType.DMA
-    q, kv, lists, stats = pl.pallas_call(
+    qm, kv, lists, stats = pl.pallas_call(
         gather_kernel,
         out_shape=(
-            jax.ShapeDtypeStruct((ROWS, D), BF),
-            jax.ShapeDtypeStruct((NB, BLOCK, 2 * D), BF),
-            jax.ShapeDtypeStruct((BLK, 128), I32),
+            jax.ShapeDtypeStruct((BLK, 2, 256, 256), BF),
+            jax.ShapeDtypeStruct((NB + 1, BLOCK, 2 * D), BF),
+            jax.ShapeDtypeStruct((56, 128), I32),
             jax.ShapeDtypeStruct((8, 128), F32),
         ),
-        in_specs=[vmem] * 7,
-        out_specs=(anywhere,) * 4,
+        in_specs=[hbm] * 7,
+        out_specs=(vmem,) * 4,
         scratch_shapes=[
+            pltpu.VMEM((ROWS, D), BF),
+            pltpu.VMEM((1, D), F32),
+            pltpu.VMEM((D, 3 * D), BF),
+            pltpu.VMEM((1, CN), I32),
+            pltpu.VMEM((NADJ, BLK), I32),
+            pltpu.VMEM((NADJ, BLK), I32),
+            pltpu.VMEM((BLK, CBLK), I32),
             pltpu.VMEM((ROWS, D), BF),
             pltpu.VMEM((4, ROWS, D), BF),
             pltpu.VMEM((2, 32, D // 2), BF),
             pltpu.VMEM((32, D // 2), BF),
             pltpu.VMEM((2, 4, 4, 4, CPAD, D // 2), BF),
-            pltpu.VMEM((NB, BLOCK, 2 * D), BF),
-            pltpu.VMEM((ROWS, D), BF),
-            pltpu.VMEM((BLK, 128), I32),
-            pltpu.VMEM((8, 128), F32),
             dma((4, 4)), dma((4, 4)), dma((2,)), dma((2,)), dma((3,)), dma((3,)),
             dma((3, 2)), dma((3, 2)), dma((3, 2)), dma((3, 2)), dma((4,)), dma((4,)),
-            dma((28,)), dma((3,)),
+            dma((7,)),
         ],
         compiler_params=pltpu.CompilerParams(
-            collective_id=0, has_side_effects=True, vmem_limit_bytes=48 * 2**20
+            collective_id=0, has_side_effects=True, vmem_limit_bytes=24 * 2**20
         ),
     )(
-        node_feats, gain_in.reshape(1, D), w_qkv, coarse_src.reshape(1, CN),
-        adjacency, fine_valid, coarse_mask,
+        *(
+            pltpu.with_memory_space_constraint(a, pltpu.HBM)
+            for a in (
+                node_feats, gain_in.reshape(1, D), w_qkv, coarse_src.reshape(1, CN),
+                adjacency.T, fine_valid.T, coarse_mask,
+            )
+        )
     )
-    smem = pl.BlockSpec(memory_space=pltpu.SMEM)
     return pl.pallas_call(
         functools.partial(attend_kernel, 8),
         out_shape=jax.ShapeDtypeStruct((ROWS, D), BF),
-        in_specs=[smem, anywhere, anywhere, vmem, vmem, vmem],
+        in_specs=[vmem, vmem, vmem, vmem, hbm, hbm],
         out_specs=vmem,
         scratch_shapes=[
-            pltpu.VMEM((ROWS, D), BF),
-            pltpu.VMEM((NB + 1, BLOCK, 2 * D), BF),
-            pltpu.VMEM((BLK + 1, 2, 256, 256), BF),
+            pltpu.SMEM((56, 128), I32),
+            pltpu.VMEM((1, D), F32),
+            pltpu.VMEM((D, D), BF),
+            pltpu.VMEM((CHUNK, D), BF),
             pltpu.VMEM((BLK + 1, 2, 256, 256), F32),
             pltpu.VMEM((BLK + 1, 2, 256, 128), F32),
-            dma((2,)),
+            dma((3,)),
         ],
-        compiler_params=pltpu.CompilerParams(vmem_limit_bytes=56 * 2**20),
-    )(lists, q, kv, stats, gain_out.reshape(1, D), w_out)
+        compiler_params=pltpu.CompilerParams(vmem_limit_bytes=28 * 2**20),
+    )(lists, qm, kv, stats, gain_out.reshape(1, D), w_out)
 
 
 def solution(mesh):

time: 258 us -> 215 us (0.83)
  the two profiles are of different devices: /device:TPU:2 before, /device:TPU:32 now
where the time goes in v2:
time: 215 us; the launch traced here: 214 us
  Pallas kernels  213 us (99%)
    pallas_call x1, Pallas kernels, per_device(): pl.pallas_call(functools.partial(attend_kernel, 8), out_shape=jax.ShapeDt...  162 us
    pallas_call x1, Pallas kernels, per_device(): pl.pallas_call(gather_kernel, out_shape=(jax.ShapeDtypeStruct((BLK, 2, 25...  51 us

profile of v2, /device:TPU:32, one launch (start us, length us, event | category | flops | bytes accessed | tf_op | source)
XLA Modules:
  0.0 214.5 jit_solution(6634901717419481577)
XLA Ops:
  0.0 51.0 %shard_map.91 = (bf16[16,2,256,256]{3,2,1,0:T(8,128)(2,1)S(1)}, bf16[121,64,1024]{2,1,0:T(8,128)(2,1)S(1)}, s32[56,128]{1,0:T(8,128)S(1)}, f32[8,128]{1,0:T(8,128)S(1)}) custom-call(bf16[1024,512]{1,0:T(8,128)(2,1)} %feats_hbm.1, f32[1,512]{1,0:T(1,128)} %bitcast.8, bf16[512,1536]{1,0:T(8,128)(2,1)} %w_hbm.2, s32[1,20]{1,0:T(1,128)} %bitcast.9, ...), custom_call_target="tpu_custom_call" | custom-call | tf_op jit(solution)/shard_map/pallas_call | solution.py:457
  51.0 0.0 copy-start
  51.0 1.0 copy-done
  52.0 0.0 copy-start.1
  52.0 0.7 copy-done.1
  52.7 161.8 %shard_map.92 = bf16[1024,512]{1,0:T(8,128)(2,1)} custom-call(s32[56,128]{1,0:T(8,128)S(1)} %get-tuple-element.9.lists_vmem, bf16[16,2,256,256]{3,2,1,0:T(8,128)(2,1)S(1)} %get-tuple-element.10.qm, bf16[121,64,1024]{2,1,0:T(8,128)(2,1)S(1)} %get-tuple-element.11.kv, f32[8,128]{1,0:T(8,128)S(1)} %get-tuple-element.12.stats, f32[1,512]{1,0:T(1,128)S(1)} %bitcast.5, ...), custom_call_target="tpu_custom_call" | custom-call | tf_op jit(solution)/shard_map/pallas_call | solution.py:496
Async XLA Ops:
  51.0 1.0 copy-start
  52.0 0.7 copy-start.1

commit v3 on v2

--- a/solution.py
+++ b/solution.py
@@ -24,6 +24,7 @@
 GRP = 4
 LOG_CAP = 60.0
 EARLY_X = ()
+RELAY_AT = 0
 LATE_X = (2, 3, 0, 1)
 BF = jnp.bfloat16
 F32 = jnp.float32
@@ -46,20 +47,22 @@
     feats_hbm, gain_hbm, w_hbm, src_hbm, adj_hbm, fine_hbm, mask_hbm,
     qm, kv, lists, stats,
     feats, gain, w, src, adj, fine, mask, normed, nbr, picked, half, ag,
-    send_n, recv_n, relay_send, a_sem, b_send, b_recv, c_send, c_recv, d_send, d_recv, e_send, e_recv, in_sem,
+    send_n, recv_n, relay_send, a_sem, b_send, b_recv, c_send, c_recv, d_send, d_recv, e_send, e_recv,
+    k_send, k_recv, f_send, f_recv, s_sem, mine_out, their, in_sem,
 ):
     r = lax.axis_index("region")
     s = lax.axis_index("sub")
     z_lo, y = r // 4, lax.rem(r, 4)
     z_hi, x, c = s // 8, lax.rem(s // 2, 4), lax.rem(s, 2)
     z = z_hi * 2 + z_lo
+    zi = z_lo * 2 + z_hi
     me = r * 16 + s
-    has = [r > 0, r < 7, s > 0, s < 15]
+    has = [r > 0, r < 7, jnp.where(c == 0, s > 0, s < 15)]
     partner = (r, s + 1 - 2 * c)
-    y_next, y_prev, y_far = (place(x, lax.rem(y + k, 4), z, c) for k in (1, 3, 2))
-    z_next, z_prev = (place(x, y, lax.rem(z + k, 4), c) for k in (1, 3))
+    y_next, y_prev = (place(x, lax.rem(y + k, 4), z, c) for k in (1, 3))
+    z_next, z_prev, z_far = (place(x, y, lax.rem(z + k, 4), c) for k in (1, 3, 2))
     x_next, x_prev = (place(lax.rem(x + k, 4), y, z, c) for k in (1, 3))
-    nbr_dev = [(r - 1, s), (r + 1, s), (r, s - 1), (r, s + 1)]
+    nbr_dev = [(r - 1, s), (r + 1, s), (r, s - 1 + 2 * c)]
 
     loads = [
         pltpu.make_async_copy(a, b, in_sem.at[i])
@@ -70,16 +73,16 @@
     for load in loads:
         load.start()
 
-    for d in range(4):
+    for d in range(3):
 
         @pl.when(jnp.logical_not(has[d]))
         def _():
             nbr[d] = jnp.zeros((ROWS, D), BF)
 
     barrier = pltpu.get_barrier_semaphore()
-    for dev in (partner, y_next, y_prev, y_far, z_next, z_prev, x_next, x_prev):
+    for dev in (partner, y_next, y_prev, z_next, z_prev, z_far, x_next, x_prev):
         pl.semaphore_signal(barrier, inc=1, device_id=dev, device_id_type=MESH)
-    for d in range(4):
+    for d in range(3):
 
         @pl.when(has[d])
         def _():
@@ -107,8 +110,11 @@
     a_copy = copy(picked.at[1 - c], half, a_sem.at[0], a_sem.at[1], partner)
     a_copy.start()
 
+    def land(d):
+        return d ^ 1 if d < 2 else 2
+
     def send_side(d, ch, dev, slot=None):
-        slot = d ^ 1 if slot is None else slot
+        slot = land(d) if slot is None else slot
         rows = pl.ds(pl.multiple_of(ch * CHUNK, CHUNK), CHUNK)
         return copy(normed.at[rows], nbr.at[slot, rows], send_n.at[d, ch], recv_n.at[slot, ch], dev)
 
@@ -118,7 +124,7 @@
 
     def side_to(d, ch):
         if d >= 2:
-            return nbr_dev[d], d ^ 1
+            return nbr_dev[d], 2
         turn = ((r == 4) if d == 0 else (r == 3)) & (ch >= 2)
         far = 0 if d == 0 else 7
         return (jnp.where(turn, far, nbr_dev[d][0]), s), jnp.where(turn, d, d ^ 1)
@@ -127,7 +133,7 @@
         for d in dirs:
             now = has[d]
             if crossing is not None:
-                over = (r == 4) if d == 0 else (r == 3)
+                over = (r == 4) if d == 0 else (r == 3) if d == 1 else (r < 0)
                 now = now & (over if crossing else jnp.logical_not(over))
 
             @pl.when(now)
@@ -148,10 +154,12 @@
     own_half = picked[c]
     lo = jnp.where(c == 0, own_half, half[...])
     hi = jnp.where(c == 0, half[...], own_half)
-    ag[c, x, z, y] = jnp.dot(pick, jnp.concatenate([lo, hi], axis=0), preferred_element_type=F32).astype(BF)
-
-    blk_ref = ag.at[c, x, z, y]
-    b_copies = [copy(blk_ref, blk_ref, b_send.at[i], b_recv.at[i], dev) for i, dev in enumerate((y_next, y_prev, y_far))]
+    block = jnp.dot(pick, jnp.concatenate([lo, hi], axis=0), preferred_element_type=F32).astype(BF)
+    for p in range(2):
+        ag[c, p, x, zi, y] = block[:, p * 128 : (p + 1) * 128]
+
+    blk_ref = ag.at[c, :, x, zi, y]
+    b_copies = [copy(blk_ref, blk_ref, b_send.at[i], b_recv.at[i], dev) for i, dev in enumerate((z_next, z_prev, z_far))]
     for b in b_copies:
         b.start()
     for ch in (3, 0, 1):
@@ -170,6 +178,10 @@
     def put_kv(vals, block, count):
         kv[pl.ds(block, count)] = vals.reshape(count, BLOCK, 2 * D)
         stats[0:1] = jnp.maximum(stats[0:1], top_norm(vals[:, :D]))
+
+    def k_copy(ch):
+        there = pl.ds((3 + c) * BLK + 4 * ch, 4)
+        return copy(kv.at[pl.ds(4 * ch, 4)], kv.at[there], k_send.at[ch], k_recv.at[ch], partner)
 
     lane_head = lax.broadcasted_iota(I32, (CHUNK, 256), 1) // HW
 
@@ -182,75 +194,62 @@
                 qh = jnp.where(lane_head == h, qv[:, g * 256 : (g + 1) * 256], jnp.zeros((), BF))
                 qm[pl.ds(4 * ch, 4), g, h * BLOCK : (h + 1) * BLOCK, :] = qh.reshape(4, BLOCK, 256)
         put_kv(jnp.dot(vals, w[:, D:], preferred_element_type=F32).astype(BF), 4 * ch, 4)
+        k_copy(ch).start()
 
     for b in b_copies:
         b.wait()
 
-    def side_part(ch, dirs):
+    def side_part(ch, dirs, crossing=None):
         for d in dirs:
-
-            @pl.when(has[d])
-            def _():
-                send_side(d ^ 1, ch, nbr_dev[d]).wait_recv()
-
-            rows = pl.ds(pl.multiple_of(ch * CHUNK, CHUNK), CHUNK)
-            vals = jnp.dot(nbr[d, rows], w[:, D:], preferred_element_type=F32).astype(BF)
-            put_kv(vals, (d + 1) * BLK + 4 * ch, 4)
-
-    def ring(slab, at, nxt, prv, snd, rcv, early, late):
-        prev_at, next_at, far_at = (lax.rem(at + k, 4) for k in (3, 1, 2))
-        to_next = [copy(slab(at, h), slab(at, h), snd.at[0, h], rcv.at[0, h], nxt) for h in range(2)]
-        to_prev = [copy(slab(at, h), slab(at, h), snd.at[1, h], rcv.at[1, h], prv) for h in range(2)]
-        for a in (to_next[0], to_prev[1], to_next[1], to_prev[0]):
-            a.start()
+            over = (r == 4) if d == 0 else (r == 3) if d == 1 else (r < 0)
+
+            def take():
+                @pl.when(has[d])
+                def _():
+                    send_side(land(d), ch, nbr_dev[d]).wait_recv()
+
+                rows = pl.ds(pl.multiple_of(ch * CHUNK, CHUNK), CHUNK)
+                vals = jnp.dot(nbr[d, rows], w[:, D:], preferred_element_type=F32).astype(BF)
+                put_kv(vals, ((d + 1) if d < 2 else (3 + c)) * BLK + 4 * ch, 4)
+
+            if crossing is None:
+                take()
+            else:
+                pl.when(over if crossing else jnp.logical_not(over))(take)
+
+    def rings(kinds, early, late):
+        sets = []
+        for slab, at, nxt, prv, snd, rcv in kinds:
+            prev_at, next_at = lax.rem(at + 3, 4), lax.rem(at + 1, 4)
+            sets.append((
+                [copy(slab(at, h), slab(at, h), snd.at[0, h], rcv.at[0, h], nxt) for h in range(2)],
+                [copy(slab(at, h), slab(at, h), snd.at[1, h], rcv.at[1, h], prv) for h in range(2)],
+                copy(slab(prev_at, 0), slab(prev_at, 0), snd.at[2, 0], rcv.at[2, 0], nxt),
+                copy(slab(next_at, 1), slab(next_at, 1), snd.at[2, 1], rcv.at[2, 1], prv),
+            ))
+        for to_next, to_prev, _, _ in sets:
+            to_next[0].start()
+            to_prev[1].start()
+        for to_next, to_prev, _, _ in sets:
+            to_next[1].start()
+            to_prev[0].start()
         early()
-        to_next[0].wait_recv()
-        on_next = copy(slab(prev_at, 0), slab(prev_at, 0), snd.at[2, 0], rcv.at[2, 0], nxt)
-        on_next.start()
-        to_prev[1].wait_recv()
-        on_prev = copy(slab(next_at, 1), slab(next_at, 1), snd.at[2, 1], rcv.at[2, 1], prv)
-        on_prev.start()
-        to_next[1].wait_recv()
-        to_prev[0].wait_recv()
-        late(prev_at, next_at)
-        on_next.wait_recv()
-        on_prev.wait_recv()
-        for a in to_next + to_prev + [on_next, on_prev]:
-            a.wait_send()
-        return far_at
-
-    def c_early():
-        def sides(i, carry):
-            start_sides((0, 1), lax.rem(i + 2, NCH), False)
-            return carry
-
-        lax.fori_loop(0, NCH, sides, 0)
-        own_chunk(0)
-
-    ring(
-        lambda i, h: ag.at[c, x, i, pl.ds(2 * h, 2)], z, z_next, z_prev, c_send, c_recv,
-        c_early, lambda p, n: None,
-    )
-
-    def e_copy(i):
-        return copy(ag.at[c, i], ag.at[c, i], e_send.at[i], e_recv.at[i], partner)
-
-    def e_start(i):
-        e_copy(i).start()
-
-    def d_early():
-        e_start(x)
-
-        def sides(i, carry):
-            start_sides((0, 1), lax.rem(i + 2, NCH), True)
-            return carry
-
-        lax.fori_loop(0, NCH, sides, 0)
-        for ch in EARLY_X:
-            start_sides((2, 3), ch)
-        own_chunk(1)
-        own_chunk(2)
-        own_chunk(3)
+        for to_next, to_prev, on_next, on_prev in sets:
+            to_next[0].wait_recv()
+            on_next.start()
+            to_prev[1].wait_recv()
+            on_prev.start()
+        for to_next, to_prev, _, _ in sets:
+            to_next[1].wait_recv()
+            to_prev[0].wait_recv()
+        late()
+        for to_next, to_prev, on_next, on_prev in sets:
+            on_next.wait_recv()
+            on_prev.wait_recv()
+            for a in to_next + to_prev + [on_next, on_prev]:
+                a.wait_send()
+
+    def find_lists():
         dev_of, local = adj[...] // BLK, lax.rem(adj[...], BLK)
         gap = dev_of - me
         side = jnp.where(gap == -16, 1, jnp.where(gap == 16, 2, jnp.where(gap == -1, 3, jnp.where(gap == 1, 4, 0))))
@@ -276,26 +275,68 @@
         lists[:, :BLK] = jnp.where(spot == 48, count, found)
         kv[NB] = jnp.zeros((BLOCK, 2 * D), BF)
 
-    def d_late(p, n):
-        e_start(p)
-        e_start(n)
-        for ch in LATE_X:
-            start_sides((2, 3), ch)
-        relay = [(7, 1, 4), (0, 0, 3)]
-        for at, d, to in relay:
+    def c_early():
+        for ch in (2, 3):
+            start_sides((0, 1), ch, True)
+        own_chunk(0)
+        find_lists()
+
+    rings(
+        [
+            (lambda i, h: ag.at[c, :, x, pl.ds(2 * h, 2), i], y, y_next, y_prev, c_send.at[0], c_recv.at[0]),
+        ],
+        c_early, lambda: None,
+    )
+
+    def e_copy(i):
+        part = ag.at[c, :, i, pl.ds(2 * (1 - c), 2)]
+        return copy(part, part, e_send.at[i], e_recv.at[i], partner)
+
+    def e_start(i):
+        e_copy(i).start()
+
+    def d_early():
+        e_start(x)
+        for ch in (0, 1):
+            start_sides((0, 1), ch, True)
+
+        def sides(i, carry):
+            start_sides((0, 1), lax.rem(i + 2, NCH), False)
+            return carry
+
+        lax.fori_loop(0, NCH, sides, 0)
+        own_chunk(1)
+        own_chunk(2)
+        own_chunk(3)
+
+    def pass_on():
+        for at, d, to in ((7, 1, 4), (0, 0, 3)):
 
             @pl.when(r == at)
             def _():
                 for ch in (2, 3):
-                    side = send_side(d ^ 1, ch, (to, s))
-                    side.wait_recv()
+                    send_side(d ^ 1, ch, (to, s)).wait_recv()
                     relay_side(d, ch, (to, s)).start()
 
-    far = ring(
-        lambda i, h: ag.at[c, i, pl.ds(2 * h, 2)], x, x_next, x_prev, d_send, d_recv, d_early, d_late
+    def d_late():
+        e_start(lax.rem(x + 3, 4))
+        e_start(lax.rem(x + 1, 4))
+        for ch in LATE_X:
+            start_sides((2,), ch)
+        if RELAY_AT == 2:
+            pass_on()
+
+    rings(
+        [
+            (lambda i, h: ag.at[c, :, i, pl.ds(2 * h, 2)], x, x_next, x_prev, d_send.at[0], d_recv.at[0]),
+        ],
+        d_early, d_late,
     )
-    e_start(far)
-    side_part(2, (0, 1))
+    e_start(lax.rem(x + 2, 4))
+    if RELAY_AT == 0:
+        pass_on()
+    if RELAY_AT < 2:
+        side_part(2, (0, 1), False)
 
     def e_wait(i, carry):
         e_copy(i).wait()
@@ -307,32 +348,57 @@
     c160 = lax.broadcasted_iota(I32, (160, 4 * CPAD), 1)
     sel = ((r160 // 40) * CPAD + lax.rem(r160, 40) == c160).astype(BF)
 
-    def coarse_part(i, carry):
-        zl, yy = i // 4, lax.rem(i, 4)
+    def f_copy(yy):
+        part = kv.at[pl.ds(WIN + 5 * (4 * c + yy), 5)]
+        return copy(part, part, f_send.at[yy], f_recv.at[yy], partner)
+
+    def coarse_part(yy, carry):
         parts = []
         for zh in range(2):
-            zz = zh * 2 + zl
-            cols = []
-            for h in range(2):
-                got = jnp.concatenate([ag[h, k, zz, yy] for k in range(4)], axis=0)
-                cols.append(jnp.dot(sel, got, preferred_element_type=F32).astype(BF))
-            parts.append(jnp.concatenate(cols, axis=1))
+            got = jnp.concatenate(
+                [
+                    jnp.concatenate([ag[h, p, k, 2 * c + zh, yy] for k in range(4)], axis=0)
+                    for h in range(2)
+                    for p in range(2)
+                ],
+                axis=1,
+            )
+            parts.append(jnp.dot(sel, got, preferred_element_type=F32).astype(BF))
         vals = jnp.concatenate(parts, axis=0)
-        put_kv(jnp.dot(vals, w[:, D:], preferred_element_type=F32).astype(BF), WIN + 5 * i, 5)
+        put_kv(jnp.dot(vals, w[:, D:], preferred_element_type=F32).astype(BF), WIN + 5 * (4 * c + yy), 5)
+        f_copy(yy).start()
         return carry
 
-    lax.fori_loop(0, 8, coarse_part, 0)
-
-    side_part(2, (2, 3))
+    lax.fori_loop(0, 4, coarse_part, 0)
+    if RELAY_AT == 1:
+        pass_on()
+    if RELAY_AT == 2:
+        side_part(2, (0, 1), False)
+    mine_out[...] = stats[...]
+    s_copy = copy(mine_out, their, s_sem.at[0], s_sem.at[1], partner)
+    s_copy.start()
+    side_part(3, (0, 1), False)
+    side_part(2, (2,))
+    side_part(3, (2,))
 
     def rest(i, carry):
-        side_part(lax.rem(i + 3, NCH), (0, 1, 2, 3))
+        side_part(i, (0, 1, 2))
         return carry
 
-    lax.fori_loop(0, NCH - 1, rest, 0)
+    lax.fori_loop(0, 2, rest, 0)
+
+    def crossed(i, carry):
+        side_part(i + 2, (0, 1), True)
+        return carry
+
+    lax.fori_loop(0, 2, crossed, 0)
+    s_copy.wait()
+    stats[...] = jnp.maximum(stats[...], their[...])
 
     def send_wait(ch, carry):
-        for d in range(4):
+        k_copy(ch).wait()
+        f_copy(ch).wait()
+        for d in range(3):
 
             @pl.when(has[d])
             def _():
@@ -473,12 +539,14 @@
             pltpu.VMEM((NADJ, BLK), I32),
             pltpu.VMEM((BLK, CBLK), I32),
             pltpu.VMEM((ROWS, D), BF),
-            pltpu.VMEM((4, ROWS, D), BF),
+            pltpu.VMEM((3, ROWS, D), BF),
             pltpu.VMEM((2, 32, D // 2), BF),
             pltpu.VMEM((32, D // 2), BF),
-            pltpu.VMEM((2, 4, 4, 4, CPAD, D // 2), BF),
-            dma((4, 4)), dma((4, 4)), dma((2,)), dma((2,)), dma((3,)), dma((3,)),
-            dma((3, 2)), dma((3, 2)), dma((3, 2)), dma((3, 2)), dma((4,)), dma((4,)),
+            pltpu.VMEM((2, 2, 4, 4, 4, CPAD, D // 4), BF),
+            dma((3, 4)), dma((3, 4)), dma((2,)), dma((2,)), dma((3,)), dma((3,)),
+            dma((1, 3, 2)), dma((1, 3, 2)), dma((1, 3, 2)), dma((1, 3, 2)), dma((4,)), dma((4,)),
+            dma((4,)), dma((4,)), dma((4,)), dma((4,)), dma((2,)),
+            pltpu.VMEM((8, 128), F32), pltpu.VMEM((8, 128), F32),
             dma((7,)),
         ],
         compiler_params=pltpu.CompilerParams(
@@ -508,7 +576,9 @@
             dma((3,)),
         ],
         compiler_params=pltpu.CompilerParams(vmem_limit_bytes=28 * 2**20),
-    )(lists, qm, kv, stats, gain_out.reshape(1, D), w_out)
+    )(lists, qm, kv, stats, *(
+        pltpu.with_memory_space_constraint(a, pltpu.HBM) for a in (gain_out.reshape(1, D), w_out)
+    ))
 
 
 def solution(mesh):

time: 215 us -> 210 us (0.977)
  the two profiles are of different devices: /device:TPU:32 before, /device:TPU:7 now
where the time goes in v3:
time: 210 us
  Pallas kernels  210 us (100%)
    pallas_call x1, Pallas kernels, per_device(): pl.pallas_call(functools.partial(attend_kernel, 8), out_shape=jax.ShapeDt...  164 us
    pallas_call x1, Pallas kernels, per_device(): pl.pallas_call(gather_kernel, out_shape=(jax.ShapeDtypeStruct((BLK, 2, 25...  45.3 us

profile of v3, /device:TPU:7, one launch (start us, length us, event | category | flops | bytes accessed | tf_op | source)
XLA Modules:
  0.0 209.7 jit_solution(13522335388407660396)
XLA Ops:
  0.0 45.3 %shard_map.91 = (bf16[16,2,256,256]{3,2,1,0:T(8,128)(2,1)S(1)}, bf16[121,64,1024]{2,1,0:T(8,128)(2,1)S(1)}, s32[56,128]{1,0:T(8,128)S(1)}, f32[8,128]{1,0:T(8,128)S(1)}) custom-call(bf16[1024,512]{1,0:T(8,128)(2,1)} %feats_hbm.1, f32[1,512]{1,0:T(1,128)} %bitcast.7, bf16[512,1536]{1,0:T(8,128)(2,1)} %w_hbm.2, s32[1,20]{1,0:T(1,128)} %bitcast.9, ...), custom_call_target="tpu_custom_call" | custom-call | tf_op jit(solution)/shard_map/pallas_call | solution.py:523
  45.4 164.3 %shard_map.92 = bf16[1024,512]{1,0:T(8,128)(2,1)} custom-call(s32[56,128]{1,0:T(8,128)S(1)} %get-tuple-element.9.lists_vmem, bf16[16,2,256,256]{3,2,1,0:T(8,128)(2,1)S(1)} %get-tuple-element.10.qm, bf16[121,64,1024]{2,1,0:T(8,128)(2,1)S(1)} %get-tuple-element.11.kv, f32[8,128]{1,0:T(8,128)S(1)} %get-tuple-element.12.stats, f32[1,512]{1,0:T(1,128)} %bitcast.8, ...), custom_call_target="tpu_custom_call" | custom-call | tf_op jit(solution)/shard_map/pallas_call | solution.py:564

commit v4 on v3

--- a/solution.py
+++ b/solution.py
@@ -22,10 +22,8 @@
 NCH = ROWS // CHUNK
 CPAD = 48
 GRP = 4
+UNROLL = 8
 LOG_CAP = 60.0
-EARLY_X = ()
-RELAY_AT = 0
-LATE_X = (2, 3, 0, 1)
 BF = jnp.bfloat16
 F32 = jnp.float32
 I32 = jnp.int32
@@ -46,7 +44,7 @@
 def gather_kernel(
     feats_hbm, gain_hbm, w_hbm, src_hbm, adj_hbm, fine_hbm, mask_hbm,
     qm, kv, lists, stats,
-    feats, gain, w, src, adj, fine, mask, normed, nbr, picked, half, ag,
+    feats, gain, w, src, adj, fine, mask, normed, nbr, picked, half, along_z, ag,
     send_n, recv_n, relay_send, a_sem, b_send, b_recv, c_send, c_recv, d_send, d_recv, e_send, e_recv,
     k_send, k_recv, f_send, f_recv, s_sem, mine_out, their, in_sem,
 ):
@@ -155,10 +153,9 @@
     lo = jnp.where(c == 0, own_half, half[...])
     hi = jnp.where(c == 0, half[...], own_half)
     block = jnp.dot(pick, jnp.concatenate([lo, hi], axis=0), preferred_element_type=F32).astype(BF)
-    for p in range(2):
-        ag[c, p, x, zi, y] = block[:, p * 128 : (p + 1) * 128]
-
-    blk_ref = ag.at[c, :, x, zi, y]
+    along_z[zi] = block
+
+    blk_ref = along_z.at[zi]
     b_copies = [copy(blk_ref, blk_ref, b_send.at[i], b_recv.at[i], dev) for i, dev in enumerate((z_next, z_prev, z_far))]
     for b in b_copies:
         b.start()
@@ -198,6 +195,12 @@
 
     for b in b_copies:
         b.wait()
+    r80 = lax.broadcasted_iota(I32, (80, 2 * CPAD), 0)
+    c80 = lax.broadcasted_iota(I32, (80, 2 * CPAD), 1)
+    tight = ((r80 // 40) * CPAD + lax.rem(r80, 40) == c80).astype(BF)
+    for h in range(2):
+        both = jnp.concatenate([along_z[2 * h], along_z[2 * h + 1]], axis=0)
+        ag[c, x, h, y] = jnp.dot(tight, both, preferred_element_type=F32).astype(BF)
 
     def side_part(ch, dirs, crossing=None):
         for d in dirs:
@@ -283,13 +286,13 @@
 
     rings(
         [
-            (lambda i, h: ag.at[c, :, x, pl.ds(2 * h, 2), i], y, y_next, y_prev, c_send.at[0], c_recv.at[0]),
+            (lambda i, h: ag.at[c, x, h, i], y, y_next, y_prev, c_send.at[0], c_recv.at[0]),
         ],
         c_early, lambda: None,
     )
 
     def e_copy(i):
-        part = ag.at[c, :, i, pl.ds(2 * (1 - c), 2)]
+        part = ag.at[c, i, 1 - c]
         return copy(part, part, e_send.at[i], e_recv.at[i], partner)
 
     def e_start(i):
@@ -321,22 +324,18 @@
     def d_late():
         e_start(lax.rem(x + 3, 4))
         e_start(lax.rem(x + 1, 4))
-        for ch in LATE_X:
+        for ch in (2, 3, 0, 1):
             start_sides((2,), ch)
-        if RELAY_AT == 2:
-            pass_on()
 
     rings(
         [
-            (lambda i, h: ag.at[c, :, i, pl.ds(2 * h, 2)], x, x_next, x_prev, d_send.at[0], d_recv.at[0]),
+            (lambda i, h: ag.at[c, i, h], x, x_next, x_prev, d_send.at[0], d_recv.at[0]),
         ],
         d_early, d_late,
     )
     e_start(lax.rem(x + 2, 4))
-    if RELAY_AT == 0:
-        pass_on()
-    if RELAY_AT < 2:
-        side_part(2, (0, 1), False)
+    pass_on()
+    side_part(2, (0, 1), False)
 
     def e_wait(i, carry):
         e_copy(i).wait()
@@ -344,36 +343,21 @@
 
     lax.fori_loop(0, 4, e_wait, 0)
 
-    r160 = lax.broadcasted_iota(I32, (160, 4 * CPAD), 0)
-    c160 = lax.broadcasted_iota(I32, (160, 4 * CPAD), 1)
-    sel = ((r160 // 40) * CPAD + lax.rem(r160, 40) == c160).astype(BF)
-
     def f_copy(yy):
         part = kv.at[pl.ds(WIN + 5 * (4 * c + yy), 5)]
         return copy(part, part, f_send.at[yy], f_recv.at[yy], partner)
 
     def coarse_part(yy, carry):
-        parts = []
-        for zh in range(2):
-            got = jnp.concatenate(
-                [
-                    jnp.concatenate([ag[h, p, k, 2 * c + zh, yy] for k in range(4)], axis=0)
-                    for h in range(2)
-                    for p in range(2)
-                ],
-                axis=1,
-            )
-            parts.append(jnp.dot(sel, got, preferred_element_type=F32).astype(BF))
-        vals = jnp.concatenate(parts, axis=0)
+        cols = []
+        for h in range(2):
+            got = [ag[h, k, c, yy] for k in range(4)]
+            cols.append(jnp.concatenate([g[40 * zh : 40 * zh + 40] for zh in range(2) for g in got], axis=0))
+        vals = jnp.concatenate(cols, axis=1)
         put_kv(jnp.dot(vals, w[:, D:], preferred_element_type=F32).astype(BF), WIN + 5 * (4 * c + yy), 5)
         f_copy(yy).start()
         return carry
 
     lax.fori_loop(0, 4, coarse_part, 0)
-    if RELAY_AT == 1:
-        pass_on()
-    if RELAY_AT == 2:
-        side_part(2, (0, 1), False)
     mine_out[...] = stats[...]
     s_copy = copy(mine_out, their, s_sem.at[0], s_sem.at[1], partner)
     s_copy.start()
@@ -415,7 +399,7 @@
                 relay_side(d, ch, (to, s)).wait_send()
 
 
-def attend_kernel(unroll, lists_vmem, qm, kv, stats, gain_hbm, w_hbm, out, lists, gain, w, mid, acc, lsum, sems):
+def attend_kernel(unroll, lists_vmem, qm, kv, stats, gain_hbm, w_hbm, out, lists, gain, w, acc, lsum, sems):
     loads = [
         pltpu.make_async_copy(a, b, sems.at[i])
         for i, (a, b) in enumerate(((lists_vmem, lists), (gain_hbm, gain), (w_hbm, w)))
@@ -441,16 +425,24 @@
     def scores(b, t, g):
         return lax.dot_general(qm[jnp.minimum(b, BLK - 1), g], blocks_of(b, t, g * 256), NT, preferred_element_type=F32)
 
-    key_lane = lax.broadcasted_iota(I32, (1, 256), 1)
+    key_lane = lax.broadcasted_iota(I32, (1, GRP * BLOCK), 1)
 
     def open_keys(b, t):
         bb = jnp.minimum(b, BLK - 1)
         return key_lane < (lists[48, bb] - t * GRP) * BLOCK
 
+    def count_up(b, g, p, keys):
+        kept = jnp.where(keys, p, 0.0)
+        lsum[b, g] += functools.reduce(
+            lambda a, e: a + e, [kept[:, i : i + 128] for i in range(0, GRP * BLOCK, 128)]
+        )
+        return p.astype(BF)
+
+    def mix(b, t, g, p):
+        acc[b, g] += jnp.dot(p, blocks_of(b, t, D + g * 256), preferred_element_type=F32)
+
     def add_up(b, t, g, p, keys):
-        kept = jnp.where(keys, p, 0.0)
-        lsum[b, g] += kept[:, :128] + kept[:, 128:]
-        acc[b, g] += jnp.dot(p.astype(BF), blocks_of(b, t, D + g * 256), preferred_element_type=F32)
+        mix(b, t, g, count_up(b, g, p, keys))
 
     @pl.when(safe)
     def _():
@@ -464,12 +456,14 @@
             spots = [at]
             for _ in range(unroll):
                 spots.append(step_on(*spots[-1]))
-            held = [scores(*spots[0], g) for g in range(2)]
-            for u in range(unroll):
-                later = [scores(*spots[u + 1], g) for g in range(2)] if u + 1 < unroll else None
-                keys = open_keys(*spots[u])
-                for g in range(2):
-                    add_up(*spots[u], g, jnp.exp(held[g]), keys)
+            steps = [(u, g) for u in range(unroll) for g in range(2)]
+            held = scores(*spots[0], 0)
+            for k, (u, g) in enumerate(steps):
+                later = None
+                if k + 1 < len(steps):
+                    nu, ng = steps[k + 1]
+                    later = scores(*spots[nu], ng)
+                add_up(*spots[u], g, jnp.exp(held), open_keys(*spots[u]))
                 held = later
             return spots[-1]
 
@@ -496,24 +490,46 @@
 
         lax.fori_loop(0, BLK, block, 0)
 
-    def finish(i, carry):
-        for k in range(4):
-            b = 4 * i + k
+    def finish(i):
+        attended = []
+        for b in range(4 * i, 4 * i + 4):
             pieces = []
             for g in range(2):
-                piece = jnp.zeros((BLOCK, 256), F32)
-                for h in range(4):
+                piece = acc[b, g, :BLOCK, :]
+                total = jnp.sum(lsum[b, g, :BLOCK, :], axis=-1, keepdims=True)
+                for h in range(1, 4):
                     rows = slice(h * BLOCK, (h + 1) * BLOCK)
-                    total = jnp.sum(lsum[b, g, rows, :], axis=-1, keepdims=True)
-                    piece = jnp.where(lane == h, acc[b, g, rows, :] / total, piece)
-                pieces.append(piece)
-            attended = jnp.concatenate(pieces, axis=1).astype(BF).astype(F32)
-            mid[k * BLOCK : (k + 1) * BLOCK] = rms(attended, gain[...])
-        rows = pl.ds(pl.multiple_of(i * CHUNK, CHUNK), CHUNK)
-        out[rows] = jnp.dot(mid[...], w[...], preferred_element_type=F32).astype(BF)
-        return carry
-
-    lax.fori_loop(0, 4, finish, 0)
+                    piece = jnp.where(lane == h, acc[b, g, rows, :], piece)
+                    total = jnp.where(lane == h, jnp.sum(lsum[b, g, rows, :], axis=-1, keepdims=True), total)
+                pieces.append(piece / total)
+            row = jnp.concatenate(pieces, axis=1).astype(BF).astype(F32)
+            attended.append(rms(row, gain[...]))
+        rows = slice(i * CHUNK, (i + 1) * CHUNK)
+        out[rows] = jnp.dot(jnp.concatenate(attended, axis=0), w[...], preferred_element_type=F32).astype(BF)
+
+    for i in range(4):
+        finish(i)
+
+
+def attend_call(lists, qm, kv, stats, gain_out, w_out):
+    vmem = pl.BlockSpec(memory_space=pltpu.VMEM)
+    hbm = pl.BlockSpec(memory_space=pltpu.HBM)
+    dma = pltpu.SemaphoreType.DMA
+    return pl.pallas_call(
+        functools.partial(attend_kernel, UNROLL),
+        out_shape=jax.ShapeDtypeStruct((ROWS, D), BF),
+        in_specs=[vmem, vmem, vmem, vmem, hbm, hbm],
+        out_specs=vmem,
+        scratch_shapes=[
+            pltpu.SMEM((56, 128), I32),
+            pltpu.VMEM((1, D), F32),
+            pltpu.VMEM((D, D), BF),
+            pltpu.VMEM((BLK + 1, 2, 256, 256), F32),
+            pltpu.VMEM((BLK + 1, 2, 256, 128), F32),
+            dma((3,)),
+        ],
+        compiler_params=pltpu.CompilerParams(vmem_limit_bytes=28 * 2**20),
+    )(lists, qm, kv, stats, gain_out, w_out)
 
 
 def per_device(node_feats, gain_in, w_qkv, gain_out, w_out, adjacency, fine_valid, coarse_mask, coarse_src):
@@ -542,7 +558,8 @@
             pltpu.VMEM((3, ROWS, D), BF),
             pltpu.VMEM((2, 32, D // 2), BF),
             pltpu.VMEM((32, D // 2), BF),
-            pltpu.VMEM((2, 2, 4, 4, 4, CPAD, D // 4), BF),
+            pltpu.VMEM((4, CPAD, D // 2), BF),
+            pltpu.VMEM((2, 4, 2, 4, 80, D // 2), BF),
             dma((3, 4)), dma((3, 4)), dma((2,)), dma((2,)), dma((3,)), dma((3,)),
             dma((1, 3, 2)), dma((1, 3, 2)), dma((1, 3, 2)), dma((1, 3, 2)), dma((4,)), dma((4,)),
             dma((4,)), dma((4,)), dma((4,)), dma((4,)), dma((2,)),
@@ -561,24 +578,10 @@
             )
         )
     )
-    return pl.pallas_call(
-        functools.partial(attend_kernel, 8),
-        out_shape=jax.ShapeDtypeStruct((ROWS, D), BF),
-        in_specs=[vmem, vmem, vmem, vmem, hbm, hbm],
-        out_specs=vmem,
-        scratch_shapes=[
-            pltpu.SMEM((56, 128), I32),
-            pltpu.VMEM((1, D), F32),
-            pltpu.VMEM((D, D), BF),
-            pltpu.VMEM((CHUNK, D), BF),
-            pltpu.VMEM((BLK + 1, 2, 256, 256), F32),
-            pltpu.VMEM((BLK + 1, 2, 256, 128), F32),
-            dma((3,)),
-        ],
-        compiler_params=pltpu.CompilerParams(vmem_limit_bytes=28 * 2**20),
-    )(lists, qm, kv, stats, *(
-        pltpu.with_memory_space_constraint(a, pltpu.HBM) for a in (gain_out.reshape(1, D), w_out)
-    ))
+    return attend_call(
+        lists, qm, kv, stats,
+        *(pltpu.with_memory_space_constraint(a, pltpu.HBM) for a in (gain_out.reshape(1, D), w_out)),
+    )
 
 
 def solution(mesh):

time: 210 us -> 211 us (level)
  the two profiles are of different devices: /device:TPU:7 before, /device:TPU:101 now
where the time goes in v4:
time: 211 us; the launch traced here: 210 us
  Pallas kernels  210 us (100%)
    pallas_call x1, Pallas kernels, attend_call(): pl.pallas_call(functools.partial(attend_kernel, UNROLL), out_shape=jax.Sh...  170 us
    pallas_call x1, Pallas kernels, per_device(): pl.pallas_call(gather_kernel, out_shape=(jax.ShapeDtypeStruct((BLK, 2, 25...  40.5 us

profile of v4, /device:TPU:101, one launch (start us, length us, event | category | flops | bytes accessed | tf_op | source)
XLA Modules:
  0.0 210.4 jit_solution(3969203900669163889)
XLA Ops:
  0.0 40.5 %shard_map.91 = (bf16[16,2,256,256]{3,2,1,0:T(8,128)(2,1)S(1)}, bf16[121,64,1024]{2,1,0:T(8,128)(2,1)S(1)}, s32[56,128]{1,0:T(8,128)S(1)}, f32[8,128]{1,0:T(8,128)S(1)}) custom-call(bf16[1024,512]{1,0:T(8,128)(2,1)} %feats_hbm.1, f32[1,512]{1,0:T(1,128)} %bitcast.7, bf16[512,1536]{1,0:T(8,128)(2,1)} %w_hbm.2, s32[1,20]{1,0:T(1,128)} %bitcast.9, ...), custom_call_target="tpu_custom_call" | custom-call | tf_op jit(solution)/shard_map/pallas_call | solution.py:539
  40.6 169.7 %shard_map.92 = bf16[1024,512]{1,0:T(8,128)(2,1)} custom-call(s32[56,128]{1,0:T(8,128)S(1)} %get-tuple-element.9.lists_vmem, bf16[16,2,256,256]{3,2,1,0:T(8,128)(2,1)S(1)} %get-tuple-element.10.qm, bf16[121,64,1024]{2,1,0:T(8,128)(2,1)S(1)} %get-tuple-element.11.kv, f32[8,128]{1,0:T(8,128)S(1)} %get-tuple-element.12.stats, f32[1,512]{1,0:T(1,128)} %bitcast.8, ...), custom_call_target="tpu_custom_call" | custom-call | tf_op jit(solution)/shard_map/pallas_call | solution.py:518

commit v5 on v4

--- a/solution.py
+++ b/solution.py
@@ -22,7 +22,7 @@
 NCH = ROWS // CHUNK
 CPAD = 48
 GRP = 4
-UNROLL = 8
+UNROLL = 10
 LOG_CAP = 60.0
 BF = jnp.bfloat16
 F32 = jnp.float32
@@ -281,6 +281,7 @@
     def c_early():
         for ch in (2, 3):
             start_sides((0, 1), ch, True)
+        start_sides((2,), 2)
         own_chunk(0)
         find_lists()
 
@@ -324,7 +325,7 @@
     def d_late():
         e_start(lax.rem(x + 3, 4))
         e_start(lax.rem(x + 1, 4))
-        for ch in (2, 3, 0, 1):
+        for ch in (3, 0, 1):
             start_sides((2,), ch)
 
     rings(
@@ -439,7 +440,11 @@
         return p.astype(BF)
 
     def mix(b, t, g, p):
-        acc[b, g] += jnp.dot(p, blocks_of(b, t, D + g * 256), preferred_element_type=F32)
+        mixed = jnp.dot(p, blocks_of(b, t, D + g * 256), preferred_element_type=F32)
+        kept = mixed[:BLOCK]
+        for h in range(1, 4):
+            kept = jnp.where(lane == h, mixed[h * BLOCK : (h + 1) * BLOCK], kept)
+        acc[b, g] += kept
 
     def add_up(b, t, g, p, keys):
         mix(b, t, g, count_up(b, g, p, keys))
@@ -495,13 +500,11 @@
         for b in range(4 * i, 4 * i + 4):
             pieces = []
             for g in range(2):
-                piece = acc[b, g, :BLOCK, :]
                 total = jnp.sum(lsum[b, g, :BLOCK, :], axis=-1, keepdims=True)
                 for h in range(1, 4):
                     rows = slice(h * BLOCK, (h + 1) * BLOCK)
-                    piece = jnp.where(lane == h, acc[b, g, rows, :], piece)
                     total = jnp.where(lane == h, jnp.sum(lsum[b, g, rows, :], axis=-1, keepdims=True), total)
-                pieces.append(piece / total)
+                pieces.append(acc[b, g] / total)
             row = jnp.concatenate(pieces, axis=1).astype(BF).astype(F32)
             attended.append(rms(row, gain[...]))
         rows = slice(i * CHUNK, (i + 1) * CHUNK)
@@ -524,7 +527,7 @@
             pltpu.SMEM((56, 128), I32),
             pltpu.VMEM((1, D), F32),
             pltpu.VMEM((D, D), BF),
-            pltpu.VMEM((BLK + 1, 2, 256, 256), F32),
+            pltpu.VMEM((BLK + 1, 2, BLOCK, 256), F32),
             pltpu.VMEM((BLK + 1, 2, 256, 128), F32),
             dma((3,)),
         ],

time: 211 us -> 205 us (0.972)
  the two profiles are of different devices: /device:TPU:101 before, /device:TPU:25 now
where the time goes in v5:
time: 205 us
  Pallas kernels  205 us (100%)
    pallas_call x1, Pallas kernels, attend_call(): pl.pallas_call(functools.partial(attend_kernel, UNROLL), out_shape=jax.Sh...  163 us
    pallas_call x1, Pallas kernels, per_device(): pl.pallas_call(gather_kernel, out_shape=(jax.ShapeDtypeStruct((BLK, 2, 25...  41.9 us

profile of v5, /device:TPU:25, one launch (start us, length us, event | category | flops | bytes accessed | tf_op | source)
XLA Modules:
  0.0 205.3 jit_solution(1679683344841725541)
XLA Ops:
  0.0 41.9 %shard_map.91 = (bf16[16,2,256,256]{3,2,1,0:T(8,128)(2,1)S(1)}, bf16[121,64,1024]{2,1,0:T(8,128)(2,1)S(1)}, s32[56,128]{1,0:T(8,128)S(1)}, f32[8,128]{1,0:T(8,128)S(1)}) custom-call(bf16[1024,512]{1,0:T(8,128)(2,1)} %feats_hbm.1, f32[1,512]{1,0:T(1,128)} %bitcast.7, bf16[512,1536]{1,0:T(8,128)(2,1)} %w_hbm.2, s32[1,20]{1,0:T(1,128)} %bitcast.9, ...), custom_call_target="tpu_custom_call" | custom-call | tf_op jit(solution)/shard_map/pallas_call | solution.py:542
  41.9 163.3 %shard_map.92 = bf16[1024,512]{1,0:T(8,128)(2,1)} custom-call(s32[56,128]{1,0:T(8,128)S(1)} %get-tuple-element.9.lists_vmem, bf16[16,2,256,256]{3,2,1,0:T(8,128)(2,1)S(1)} %get-tuple-element.10.qm, bf16[121,64,1024]{2,1,0:T(8,128)(2,1)S(1)} %get-tuple-element.11.kv, f32[8,128]{1,0:T(8,128)S(1)} %get-tuple-element.12.stats, f32[1,512]{1,0:T(1,128)} %bitcast.8, ...), custom_call_target="tpu_custom_call" | custom-call | tf_op jit(solution)/shard_map/pallas_call | solution.py:521

commit v6 on v5

--- a/solution.py
+++ b/solution.py
@@ -22,7 +22,7 @@
 NCH = ROWS // CHUNK
 CPAD = 48
 GRP = 4
-UNROLL = 10
+UNROLL = 16
 LOG_CAP = 60.0
 BF = jnp.bfloat16
 F32 = jnp.float32

time: 205 us -> 204 us (level)
  the two profiles are of different devices: /device:TPU:25 before, /device:TPU:61 now
where the time goes in v6:
time: 204 us; the launch traced here: 203 us
  Pallas kernels  203 us (100%)
    pallas_call x1, Pallas kernels, attend_call(): pl.pallas_call(functools.partial(attend_kernel, UNROLL), out_shape=jax.Sh...  165 us
    pallas_call x1, Pallas kernels, per_device(): pl.pallas_call(gather_kernel, out_shape=(jax.ShapeDtypeStruct((BLK, 2, 25...  38.3 us

profile of v6, /device:TPU:61, one launch (start us, length us, event | category | flops | bytes accessed | tf_op | source)
XLA Modules:
  0.0 203.2 jit_solution(4357866626230709287)
XLA Ops:
  0.0 38.3 %shard_map.91 = (bf16[16,2,256,256]{3,2,1,0:T(8,128)(2,1)S(1)}, bf16[121,64,1024]{2,1,0:T(8,128)(2,1)S(1)}, s32[56,128]{1,0:T(8,128)S(1)}, f32[8,128]{1,0:T(8,128)S(1)}) custom-call(bf16[1024,512]{1,0:T(8,128)(2,1)} %feats_hbm.1, f32[1,512]{1,0:T(1,128)} %bitcast.7, bf16[512,1536]{1,0:T(8,128)(2,1)} %w_hbm.2, s32[1,20]{1,0:T(1,128)} %bitcast.9, ...), custom_call_target="tpu_custom_call" | custom-call | tf_op jit(solution)/shard_map/pallas_call | solution.py:542
  38.3 164.7 %shard_map.92 = bf16[1024,512]{1,0:T(8,128)(2,1)} custom-call(s32[56,128]{1,0:T(8,128)S(1)} %get-tuple-element.9.lists_vmem, bf16[16,2,256,256]{3,2,1,0:T(8,128)(2,1)S(1)} %get-tuple-element.10.qm, bf16[121,64,1024]{2,1,0:T(8,128)(2,1)S(1)} %get-tuple-element.11.kv, f32[8,128]{1,0:T(8,128)S(1)} %get-tuple-element.12.stats, f32[1,512]{1,0:T(1,128)} %bitcast.8, ...), custom_call_target="tpu_custom_call" | custom-call | tf_op jit(solution)/shard_map/pallas_call | solution.py:521
